TPU v7x, 128 devices: a whole 4x4x4 slice. The times are simulated.
128 devices in a mesh: view: 16 (over x, y), tok: 8 (over z, core).
Axes of the slice: x: 4, y: 4, z: 4, core: 2. Of those that a mesh axis runs over, the one named last changes fastest.
Arguments:
- x_target: bfloat16 [16, 4096, 1024], P('view', 'tok'), may hold values from -50 to 50
- cond_x: bfloat16 [2048, 1024], P(('view', 'tok')), may hold values from -50 to 50
- w_query: bfloat16 [1024, 1024], replicated, may hold values from -1 to 1
- w_key: bfloat16 [1024, 1024], replicated, may hold values from -1 to 1
- w_value: bfloat16 [1024, 1024], replicated, may hold values from -0.1875 to 0.1875
- w_out: bfloat16 [1024, 1024], replicated, may hold values from -0.1875 to 0.1875
- epi_lists: int32 [16, 32, 8, 2], P('view', 'tok'), may hold values from -1 to 31, as said below
Outputs:
- mixed: bfloat16 [16, 4096, 1024], P('view', 'tok')
Inputs may be any that keep to these rules, and one draw needn't show every extreme that they name: `epi_lists`: each query block in row band t (blocks t * 4 onward) names only key blocks of bands t - 1, t, t + 1; pairs of one query block are distinct and its used entries come first. Over the query blocks of one band of one view, at most 2 distinct key blocks of any one view are named, and in every band of every view some view has exactly 2; one query block of each band names 8 pairs.
All inputs are finite; a program needn't handle non-finite values.
Results may differ from a plain program's by a relative error of at most 0.012.
Values may be sent and summed in bfloat16 or wider, within the bound.
A program may use at most 192 MiB of HBM per device.

v0:
```python
import jax
import jax.numpy as jnp
from jax import lax
from jax.sharding import PartitionSpec as P

HD = 64
BLK = 128
CAP = 2


def extended(x, sides, width):
    for axis, dim in sides:
        peers, length = (lax.axis_size(axis), x.shape[dim])
        up = [(i, (i + 1) % peers) for i in range(peers - 1)]
        down = [(j, i) for i, j in up]
        last = lax.slice_in_dim(x, length - width, length, axis=dim)
        initial = lax.slice_in_dim(x, 0, width, axis=dim)
        before = lax.ppermute(last, axis, up)
        after = lax.ppermute(initial, axis, down)
        x = jnp.concatenate([before, x, after], axis=dim)
    return x


def attend(carry, query_heads, keyset, valueset, bias):
    peak, total, accum = carry
    count = keyset.shape[0]
    heads = query_heads.shape[1]
    key_heads = keyset.reshape(count, heads, HD)
    value_heads = valueset.reshape(count, heads, HD)
    scores = jnp.einsum(
        "qhd,khd->qhk", query_heads, key_heads, preferred_element_type=jnp.float32
    ) * HD ** (-0.5)
    if bias is not None:
        scores = scores + bias[:, None, :]
    fresh = jnp.maximum(peak, jnp.max(scores, axis=-1))
    factor = jnp.exp(peak - fresh)
    weights = jnp.exp(scores - fresh[..., None])
    total = total * factor + jnp.sum(weights, axis=-1)
    accum = accum * factor[..., None] + jnp.einsum(
        "qhk,khd->qhd",
        weights.astype(jnp.bfloat16),
        value_heads,
        preferred_element_type=jnp.float32,
    )
    return (fresh, total, accum)


def attend_panel(carry, query_heads, pair):
    count = pair.shape[0]
    blocks = pair.reshape(count // 512, 512, 2, pair.shape[2])

    def attend_step(state, piece):
        return (attend(state, query_heads, piece[:, 0], piece[:, 1], None), None)

    carry, _ = lax.scan(attend_step, carry, blocks)
    return carry


def local(x_target, cond_x, w_query, w_key, w_value, w_out, epi_lists):
    rows = x_target.shape[1]
    width = x_target.shape[2]
    heads = width // HD
    tokens = x_target[0]
    query_heads = (
        jnp.dot(tokens, w_query, preferred_element_type=jnp.float32)
        .astype(jnp.bfloat16)
        .reshape(rows, heads, HD)
    )
    key_rows = jnp.dot(tokens, w_key, preferred_element_type=jnp.float32).astype(jnp.bfloat16)
    value_rows = jnp.dot(tokens, w_value, preferred_element_type=jnp.float32).astype(jnp.bfloat16)
    band_pair = jnp.stack([key_rows, value_rows], axis=1)
    initial = (
        jnp.full((rows, heads), -1e30, jnp.float32),
        jnp.zeros((rows, heads), jnp.float32),
        jnp.zeros((rows, heads, HD), jnp.float32),
    )
    cond_keys = jnp.dot(cond_x, w_key, preferred_element_type=jnp.float32).astype(jnp.bfloat16)
    cond_values = jnp.dot(cond_x, w_value, preferred_element_type=jnp.float32).astype(jnp.bfloat16)
    cond_pair = jnp.stack([cond_keys, cond_values], axis=1)
    carry = attend_panel(
        initial, query_heads, lax.all_gather(cond_pair, ("view", "tok"), axis=0, tiled=True)
    )
    nview = lax.axis_size("view")
    band = lax.axis_index("tok")
    per_band = rows // BLK
    span = 3 * per_band
    lists = epi_lists[0]
    view_entry = lists[..., 0]
    block_entry = lists[..., 1]
    valid = view_entry >= 0
    local_entry = block_entry - (band - 1) * per_band
    view_hit = (view_entry[..., None] == jnp.arange(nview)).astype(jnp.float32)
    local_hit = ((local_entry[..., None] == jnp.arange(span)) & valid[..., None]).astype(
        jnp.float32
    )
    present = (jnp.einsum("bmv,bmw->vw", view_hit, local_hit) > 0.5).astype(jnp.int32)
    ranking = jnp.cumsum(present, axis=1) - present
    picked = (present[:, None, :] > 0) & (ranking[:, None, :] == jnp.arange(CAP)[None, :, None])
    request = jnp.where(jnp.any(picked, axis=-1), jnp.sum(picked * jnp.arange(span), axis=-1), -1)
    slot_entry = jnp.einsum(
        "bmv,bmw,vw->bm", view_hit, local_hit, ranking.astype(jnp.float32)
    ).astype(jnp.int32)
    incoming = lax.all_to_all(request, "view", split_axis=0, concat_axis=0, tiled=True)
    window = extended(band_pair, (("tok", 0),), rows)
    window_blocks = window.reshape(span, BLK, 2, width)
    wanted = jnp.take(window_blocks, jnp.clip(incoming, 0, span - 1), axis=0)
    wanted = jnp.where((incoming >= 0)[:, :, None, None, None], wanted, jnp.zeros_like(wanted))
    received = lax.all_to_all(wanted, "view", split_axis=0, concat_axis=0, tiled=True)
    pool_size = nview * CAP
    pool_entry = jnp.clip(view_entry, 0) * CAP + slot_entry
    slot_mask = jnp.any((pool_entry[..., None] == jnp.arange(pool_size)) & valid[..., None], axis=1)
    group = max(1, 512 // BLK)
    steps_count = pool_size // group
    key_groups = received.reshape(steps_count, group * BLK, 2, width)
    mask_groups = jnp.transpose(slot_mask.reshape(per_band, steps_count, group), (1, 0, 2))

    def body_step(state, inputs):
        piece, mask_piece = inputs
        row_mask = jnp.repeat(jnp.repeat(mask_piece, BLK, axis=0), BLK, axis=1)
        bias = jnp.where(row_mask, 0.0, -1e30).astype(jnp.float32)
        return (attend(state, query_heads, piece[:, 0], piece[:, 1], bias), None)

    carry, _ = lax.scan(body_step, carry, (key_groups, mask_groups))
    peak, total, accum = carry
    attended = (accum / total[..., None]).reshape(rows, width).astype(jnp.bfloat16)
    mixed = jnp.dot(attended, w_out, preferred_element_type=jnp.float32).astype(jnp.bfloat16)
    return mixed[None]


def solution(mesh):
    placed = (
        P("view", "tok", None),
        P(("view", "tok"), None),
        P(),
        P(),
        P(),
        P(),
        P("view", "tok", None, None),
    )
    return jax.shard_map(
        local, mesh=mesh, in_specs=placed, out_specs=P("view", "tok", None), check_vma=False
    )
```

profile of v0, /device:TPU:33, one launch (start us, length us, event | category | flops | bytes accessed | tf_op | source)
XLA Modules:
  0.0 691.4 jit_solution(908966842132727105)
XLA Ops:
  22.9 13.0 %all_to_all.11 = s32[16,1,2]{2,1,0:T(1,128)S(1)} all-to-all(s32[16,1,2]{2,1,0:T(1,128)S(1)} %copy.93), channel_id=1, replica_groups=mesh['view'=16,'tok'=8] {'view'}, dimensions={0} | all-to-all | bytes 256 | tf_op jit(solution)/shard_map/all_to_all | solution.py:103
  36.4 8.8 %collective-permute-done.1 = bf16[512,2,1024]{2,0,1:T(8,128)(2,1)} collective-permute-done((bf16[512,2,1024]{2,0,1:T(8,128)(2,1)}, bf16[512,2,1024]{2,0,1:T(8,128)(2,1)}, u32[]{:S(2)}, u32[]{:S(2)}) %collective-permute-start.1) | collective-permute-done | bytes 2097184 | tf_op jit(solution)/shard_map/ppermute | solution.py:19
  47.0 5.5 pad_maximum_fusion
  52.5 9.9 %gather_fusion = bf16[32,128,2,1024]{3,1,2,0:T(8,128)(2,1)} fusion(bf16[12,128,2,1024]{3,1,0,2:T(8,128)(2,1)} %bitcast.176, s32[1024]{0:T(1024)S(1)} %pad_clamp_fusion), kind=kCustom, calls=%fused_computation | custom fusion | bytes 33554560 | tf_op jit(solution)/shard_map/jit(_take)/gather | solution.py:106
  62.4 9.6 %select_select_fusion = bf16[16,2,128,2,1024]{4,2,3,1,0:T(8,128)(2,1)S(1)} fusion(bf16[16,2,128,2,1024]{4,2,3,1,0:T(8,128)(2,1)} %bitcast.177, pred[16,2]{1,0:T(8,128)(4,1)S(1)} %copy.97, pred[16,2]{1,0:T(8,128)(4,1)S(1)} %copy.95), kind=kLoop, calls=%fused_computation.31 | loop fusion | flops 16777216 | bytes 33554496 | tf_op jit(solution)/shard_map/jit(_where)/select_n | solution.py:107
  72.0 6.7 copy.99
  78.8 7.4 %all-to-all-start.1 = ((bf16[16,2,128,2,1024]{4,2,1,3,0:T(8,128)(2,1)}), bf16[16,2,128,2,1024]{4,2,1,3,0:T(8,128)(2,1)}, u32[]{:S(2)}, u32[]{:S(2)}) async-start(bf16[16,2,128,2,1024]{4,2,1,3,0:T(8,128)(2,1)} %copy.99), calls=%async_computation.1 | async-start | bytes 33554432 | tf_op jit(solution)/shard_map/all_to_all | solution.py:108
  90.2 134.1 %while.30 = (s32[]{:T(128)}, f32[512,16]{0,1:T(8,128)S(1)}, f32[512,16]{0,1:T(8,128)S(1)}, f32[512,16,64]{0,2,1:T(8,128)}, bf16[4,512,2,1024]{3,1,0,2:T(8,128)(2...) while((s32[]{:T(128)}, f32[512,16]{0,1:T(8,128)S(1)}, f32[512,16]{0,1:T(8,128)S(1)}, ...), condition=%wide.region_3.4_spmd.clone, body=%wide.region_0.3_spmd.clone.sunk | while | flops 1108910080 | bytes 70778984 | solution.py:55
  96.3 8.1 %bitcast_reduce_fusion.2 = (f32[512,16]{0,1:T(8,128)S(1)}, f32[16,512,512]{2,1,0:T(8,128)}) fusion(bf16[512,16,64]{0,2,1:T(8,128)(2,1)S(1)} %bitcast.174, bf16[512,16,64]{0,2,1:T(8,128)(2,1)S(1)} %get-tuple-element.348), kind=kOutput, calls=%fused_computation.16.clone.1 | convolution fusion | flops 545251328 | bytes 18907136 | tf_op jit(solution)/shard_map/while/body/eval_jaxpr/qhd,khd->qhk/dot_general | solution.py:30
  104.4 8.6 %fusion.86 = f32[512,16]{0,1:T(8,128)S(1)} fusion(f32[16,512,512]{2,1,0:T(8,128)} %get-tuple-element.323, f32[512,16]{0,1:T(8,128)S(1)} %select_maximum_fusion.2), kind=kLoop, calls=%fused_computation.19.clone.1 | loop fusion | flops 12574720 | bytes 16842752 | tf_op jit(solution)/shard_map/while/body/eval_jaxpr/reduce_sum | solution.py:38
  113.0 10.3 %bitcast_add_fusion.6 = f32[512,16,64]{0,2,1:T(8,128)} fusion(f32[512,16,64]{0,2,1:T(8,128)} %get-tuple-element.338, bf16[512,16,64]{0,2,1:T(8,128)(2,1)S(1)} %bitcast.172, f32[16,512,512]{2,1,0:T(8,128)} %get-tuple-element.323, f32[512,16]{0,1:T(8,128)S(1)} %select_maximum_fusion.2, f32[512,16]{0,1:T(8,128)S(1)} %get-tuple-element.326, pred[]{:T(512)S(6)} %compare.3), kind=kOutput, calls=%fused_computation.23.clone.1 | convolution fusion | flops 551026688 | bytes 22085632 | tf_op jit(solution)/shard_map/while/body/eval_jaxpr/qhk,khd->qhd/dot_general | solution.py:39
  129.3 8.1 %bitcast_reduce_fusion.2 = (f32[512,16]{0,1:T(8,128)S(1)}, f32[16,512,512]{2,1,0:T(8,128)}) fusion(bf16[512,16,64]{0,2,1:T(8,128)(2,1)S(1)} %bitcast.174, bf16[512,16,64]{0,2,1:T(8,128)(2,1)S(1)} %get-tuple-element.348), kind=kOutput, calls=%fused_computation.16.clone.1 | convolution fusion | flops 545251328 | bytes 18907136 | tf_op jit(solution)/shard_map/while/body/eval_jaxpr/qhd,khd->qhk/dot_general | solution.py:30
  137.4 8.6 %fusion.86 = f32[512,16]{0,1:T(8,128)S(1)} fusion(f32[16,512,512]{2,1,0:T(8,128)} %get-tuple-element.323, f32[512,16]{0,1:T(8,128)S(1)} %select_maximum_fusion.2), kind=kLoop, calls=%fused_computation.19.clone.1 | loop fusion | flops 12574720 | bytes 16842752 | tf_op jit(solution)/shard_map/while/body/eval_jaxpr/reduce_sum | solution.py:38
  146.0 10.9 %bitcast_add_fusion.6 = f32[512,16,64]{0,2,1:T(8,128)} fusion(f32[512,16,64]{0,2,1:T(8,128)} %get-tuple-element.338, bf16[512,16,64]{0,2,1:T(8,128)(2,1)S(1)} %bitcast.172, f32[16,512,512]{2,1,0:T(8,128)} %get-tuple-element.323, f32[512,16]{0,1:T(8,128)S(1)} %select_maximum_fusion.2, f32[512,16]{0,1:T(8,128)S(1)} %get-tuple-element.326, pred[]{:T(512)S(6)} %compare.3), kind=kOutput, calls=%fused_computation.23.clone.1 | convolution fusion | flops 551026688 | bytes 22085632 | tf_op jit(solution)/shard_map/while/body/eval_jaxpr/qhk,khd->qhd/dot_general | solution.py:39
  163.0 8.1 %bitcast_reduce_fusion.2 = (f32[512,16]{0,1:T(8,128)S(1)}, f32[16,512,512]{2,1,0:T(8,128)}) fusion(bf16[512,16,64]{0,2,1:T(8,128)(2,1)S(1)} %bitcast.174, bf16[512,16,64]{0,2,1:T(8,128)(2,1)S(1)} %get-tuple-element.348), kind=kOutput, calls=%fused_computation.16.clone.1 | convolution fusion | flops 545251328 | bytes 18907136 | tf_op jit(solution)/shard_map/while/body/eval_jaxpr/qhd,khd->qhk/dot_general | solution.py:30
  171.1 8.6 %fusion.86 = f32[512,16]{0,1:T(8,128)S(1)} fusion(f32[16,512,512]{2,1,0:T(8,128)} %get-tuple-element.323, f32[512,16]{0,1:T(8,128)S(1)} %select_maximum_fusion.2), kind=kLoop, calls=%fused_computation.19.clone.1 | loop fusion | flops 12574720 | bytes 16842752 | tf_op jit(solution)/shard_map/while/body/eval_jaxpr/reduce_sum | solution.py:38
  179.7 10.9 %bitcast_add_fusion.6 = f32[512,16,64]{0,2,1:T(8,128)} fusion(f32[512,16,64]{0,2,1:T(8,128)} %get-tuple-element.338, bf16[512,16,64]{0,2,1:T(8,128)(2,1)S(1)} %bitcast.172, f32[16,512,512]{2,1,0:T(8,128)} %get-tuple-element.323, f32[512,16]{0,1:T(8,128)S(1)} %select_maximum_fusion.2, f32[512,16]{0,1:T(8,128)S(1)} %get-tuple-element.326, pred[]{:T(512)S(6)} %compare.3), kind=kOutput, calls=%fused_computation.23.clone.1 | convolution fusion | flops 551026688 | bytes 22085632 | tf_op jit(solution)/shard_map/while/body/eval_jaxpr/qhk,khd->qhd/dot_general | solution.py:39
  196.7 8.1 %bitcast_reduce_fusion.2 = (f32[512,16]{0,1:T(8,128)S(1)}, f32[16,512,512]{2,1,0:T(8,128)}) fusion(bf16[512,16,64]{0,2,1:T(8,128)(2,1)S(1)} %bitcast.174, bf16[512,16,64]{0,2,1:T(8,128)(2,1)S(1)} %get-tuple-element.348), kind=kOutput, calls=%fused_computation.16.clone.1 | convolution fusion | flops 545251328 | bytes 18907136 | tf_op jit(solution)/shard_map/while/body/eval_jaxpr/qhd,khd->qhk/dot_general | solution.py:30
  204.8 8.6 %fusion.86 = f32[512,16]{0,1:T(8,128)S(1)} fusion(f32[16,512,512]{2,1,0:T(8,128)} %get-tuple-element.323, f32[512,16]{0,1:T(8,128)S(1)} %select_maximum_fusion.2), kind=kLoop, calls=%fused_computation.19.clone.1 | loop fusion | flops 12574720 | bytes 16842752 | tf_op jit(solution)/shard_map/while/body/eval_jaxpr/reduce_sum | solution.py:38
  213.4 10.9 %bitcast_add_fusion.6 = f32[512,16,64]{0,2,1:T(8,128)} fusion(f32[512,16,64]{0,2,1:T(8,128)} %get-tuple-element.338, bf16[512,16,64]{0,2,1:T(8,128)(2,1)S(1)} %bitcast.172, f32[16,512,512]{2,1,0:T(8,128)} %get-tuple-element.323, f32[512,16]{0,1:T(8,128)S(1)} %select_maximum_fusion.2, f32[512,16]{0,1:T(8,128)S(1)} %get-tuple-element.326, pred[]{:T(512)S(6)} %compare.3), kind=kOutput, calls=%fused_computation.23.clone.1 | convolution fusion | flops 551026688 | bytes 22085632 | tf_op jit(solution)/shard_map/while/body/eval_jaxpr/qhk,khd->qhd/dot_general | solution.py:39
  224.3 159.7 %all-to-all-done.1 = bf16[16,2,128,2,1024]{4,2,1,3,0:T(8,128)(2,1)} async-done(((bf16[16,2,128,2,1024]{4,2,1,3,0:T(8,128)(2,1)}), bf16[16,2,128,2,1024]{4,2,1,3,0:T(8,128)(2,1)}, u32[]{:S(2)}, u32[]{:S(2)}) %all-to-all-start.1) | async-done | bytes 16777248 | tf_op jit(solution)/shard_map/all_to_all | solution.py:108
  384.0 13.9 %copy.100 = bf16[16,2,128,2,1024]{4,2,1,0,3:T(8,128)(2,1)} copy(bf16[16,2,128,2,1024]{4,2,1,3,0:T(8,128)(2,1)} %all-to-all-done.1) | data formatting | bytes 33554432 | tf_op jit(solution)/shard_map/all_to_all | solution.py:108
  397.9 280.8 %while.29 = (s32[]{:T(128)}, f32[512,16]{0,1:T(8,128)S(1)}, f32[512,16]{0,1:T(8,128)S(1)}, f32[512,16,64]{0,2,1:T(8,128)}, bf16[8,512,2,1024]{3,1,0,2:T(8,128)(2...) while((s32[]{:T(128)}, f32[512,16]{0,1:T(8,128)S(1)}, ...), condition=%wide.region_11.12_spmd, body=%wide.region_8.11_spmd.sunk | while | flops 1120944128 | bytes 75006328 | solution.py:123
  406.9 7.0 %fusion.79 = (f32[512,16]{0,1:T(8,128)S(1)}, f32[16,512,512]{2,1,0:T(8,128)}) fusion(f32[512,512]{0,1:T(8,128)S(1)} %bitcast.166, bf16[512,16,64]{0,2,1:T(8,128)(2,1)S(1)} %bitcast.175, bf16[512,16,64]{0,2,1:T(8,128)(2,1)S(1)} %get-tuple-element.372), kind=kOutput, calls=%fused_computation.5.clone.1 | convolution fusion | flops 549445632 | bytes 19955712 | tf_op jit(solution)/shard_map/while/body/eval_jaxpr/qhd,khd->qhk/dot_general | solution.py:30
  414.0 9.1 %fusion.80 = f32[512,16]{0,1:T(8,128)S(1)} fusion(f32[16,512,512]{2,1,0:T(8,128)} %get-tuple-element.311, f32[512,16]{0,1:T(8,128)S(1)} %max.22, f32[512,512]{0,1:T(8,128)S(1)} %bitcast.167), kind=kLoop, calls=%fused_computation.4.clone.1 | loop fusion | flops 16769024 | bytes 17891328 | tf_op jit(solution)/shard_map/while/body/eval_jaxpr/reduce_sum | solution.py:38
  423.1 9.9 %bitcast_add_fusion.5 = f32[512,16,64]{0,2,1:T(8,128)} fusion(f32[512,16,64]{0,2,1:T(8,128)} %get-tuple-element.362, bf16[512,16,64]{0,2,1:T(8,128)(2,1)S(1)} %bitcast.173, f32[16,512,512]{2,1,0:T(8,128)} %get-tuple-element.311, f32[512,16]{0,1:T(8,128)S(1)} %max.22, f32[512,512]{0,1:T(8,128)S(1)} %bitcast.168, f32[512,16]{0,1:T(8,128)S(1)} %get-tuple-element.314), kind=kOutput, calls=%fused_computation.7.clone.1 | convolution fusion | flops 554696704 | bytes 23134208 | tf_op jit(solution)/shard_map/while/body/eval_jaxpr/qhk,khd->qhd/dot_general | solution.py:39
  436.4 3.9 copy.124
  442.0 7.0 %fusion.79 = (f32[512,16]{0,1:T(8,128)S(1)}, f32[16,512,512]{2,1,0:T(8,128)}) fusion(f32[512,512]{0,1:T(8,128)S(1)} %bitcast.166, bf16[512,16,64]{0,2,1:T(8,128)(2,1)S(1)} %bitcast.175, bf16[512,16,64]{0,2,1:T(8,128)(2,1)S(1)} %get-tuple-element.372), kind=kOutput, calls=%fused_computation.5.clone.1 | convolution fusion | flops 549445632 | bytes 19955712 | tf_op jit(solution)/shard_map/while/body/eval_jaxpr/qhd,khd->qhk/dot_general | solution.py:30
  449.1 9.1 %fusion.80 = f32[512,16]{0,1:T(8,128)S(1)} fusion(f32[16,512,512]{2,1,0:T(8,128)} %get-tuple-element.311, f32[512,16]{0,1:T(8,128)S(1)} %max.22, f32[512,512]{0,1:T(8,128)S(1)} %bitcast.167), kind=kLoop, calls=%fused_computation.4.clone.1 | loop fusion | flops 16769024 | bytes 17891328 | tf_op jit(solution)/shard_map/while/body/eval_jaxpr/reduce_sum | solution.py:38
  458.2 9.9 %bitcast_add_fusion.5 = f32[512,16,64]{0,2,1:T(8,128)} fusion(f32[512,16,64]{0,2,1:T(8,128)} %get-tuple-element.362, bf16[512,16,64]{0,2,1:T(8,128)(2,1)S(1)} %bitcast.173, f32[16,512,512]{2,1,0:T(8,128)} %get-tuple-element.311, f32[512,16]{0,1:T(8,128)S(1)} %max.22, f32[512,512]{0,1:T(8,128)S(1)} %bitcast.168, f32[512,16]{0,1:T(8,128)S(1)} %get-tuple-element.314), kind=kOutput, calls=%fused_computation.7.clone.1 | convolution fusion | flops 554696704 | bytes 23134208 | tf_op jit(solution)/shard_map/while/body/eval_jaxpr/qhk,khd->qhd/dot_general | solution.py:39
  477.1 7.0 %fusion.79 = (f32[512,16]{0,1:T(8,128)S(1)}, f32[16,512,512]{2,1,0:T(8,128)}) fusion(f32[512,512]{0,1:T(8,128)S(1)} %bitcast.166, bf16[512,16,64]{0,2,1:T(8,128)(2,1)S(1)} %bitcast.175, bf16[512,16,64]{0,2,1:T(8,128)(2,1)S(1)} %get-tuple-element.372), kind=kOutput, calls=%fused_computation.5.clone.1 | convolution fusion | flops 549445632 | bytes 19955712 | tf_op jit(solution)/shard_map/while/body/eval_jaxpr/qhd,khd->qhk/dot_general | solution.py:30
  484.2 9.1 %fusion.80 = f32[512,16]{0,1:T(8,128)S(1)} fusion(f32[16,512,512]{2,1,0:T(8,128)} %get-tuple-element.311, f32[512,16]{0,1:T(8,128)S(1)} %max.22, f32[512,512]{0,1:T(8,128)S(1)} %bitcast.167), kind=kLoop, calls=%fused_computation.4.clone.1 | loop fusion | flops 16769024 | bytes 17891328 | tf_op jit(solution)/shard_map/while/body/eval_jaxpr/reduce_sum | solution.py:38
  493.3 9.9 %bitcast_add_fusion.5 = f32[512,16,64]{0,2,1:T(8,128)} fusion(f32[512,16,64]{0,2,1:T(8,128)} %get-tuple-element.362, bf16[512,16,64]{0,2,1:T(8,128)(2,1)S(1)} %bitcast.173, f32[16,512,512]{2,1,0:T(8,128)} %get-tuple-element.311, f32[512,16]{0,1:T(8,128)S(1)} %max.22, f32[512,512]{0,1:T(8,128)S(1)} %bitcast.168, f32[512,16]{0,1:T(8,128)S(1)} %get-tuple-element.314), kind=kOutput, calls=%fused_computation.7.clone.1 | convolution fusion | flops 554696704 | bytes 23134208 | tf_op jit(solution)/shard_map/while/body/eval_jaxpr/qhk,khd->qhd/dot_general | solution.py:39
  512.2 7.0 %fusion.79 = (f32[512,16]{0,1:T(8,128)S(1)}, f32[16,512,512]{2,1,0:T(8,128)}) fusion(f32[512,512]{0,1:T(8,128)S(1)} %bitcast.166, bf16[512,16,64]{0,2,1:T(8,128)(2,1)S(1)} %bitcast.175, bf16[512,16,64]{0,2,1:T(8,128)(2,1)S(1)} %get-tuple-element.372), kind=kOutput, calls=%fused_computation.5.clone.1 | convolution fusion | flops 549445632 | bytes 19955712 | tf_op jit(solution)/shard_map/while/body/eval_jaxpr/qhd,khd->qhk/dot_general | solution.py:30
  519.3 9.1 %fusion.80 = f32[512,16]{0,1:T(8,128)S(1)} fusion(f32[16,512,512]{2,1,0:T(8,128)} %get-tuple-element.311, f32[512,16]{0,1:T(8,128)S(1)} %max.22, f32[512,512]{0,1:T(8,128)S(1)} %bitcast.167), kind=kLoop, calls=%fused_computation.4.clone.1 | loop fusion | flops 16769024 | bytes 17891328 | tf_op jit(solution)/shard_map/while/body/eval_jaxpr/reduce_sum | solution.py:38
  528.4 9.9 %bitcast_add_fusion.5 = f32[512,16,64]{0,2,1:T(8,128)} fusion(f32[512,16,64]{0,2,1:T(8,128)} %get-tuple-element.362, bf16[512,16,64]{0,2,1:T(8,128)(2,1)S(1)} %bitcast.173, f32[16,512,512]{2,1,0:T(8,128)} %get-tuple-element.311, f32[512,16]{0,1:T(8,128)S(1)} %max.22, f32[512,512]{0,1:T(8,128)S(1)} %bitcast.168, f32[512,16]{0,1:T(8,128)S(1)} %get-tuple-element.314), kind=kOutput, calls=%fused_computation.7.clone.1 | convolution fusion | flops 554696704 | bytes 23134208 | tf_op jit(solution)/shard_map/while/body/eval_jaxpr/qhk,khd->qhd/dot_general | solution.py:39
  547.3 7.0 %fusion.79 = (f32[512,16]{0,1:T(8,128)S(1)}, f32[16,512,512]{2,1,0:T(8,128)}) fusion(f32[512,512]{0,1:T(8,128)S(1)} %bitcast.166, bf16[512,16,64]{0,2,1:T(8,128)(2,1)S(1)} %bitcast.175, bf16[512,16,64]{0,2,1:T(8,128)(2,1)S(1)} %get-tuple-element.372), kind=kOutput, calls=%fused_computation.5.clone.1 | convolution fusion | flops 549445632 | bytes 19955712 | tf_op jit(solution)/shard_map/while/body/eval_jaxpr/qhd,khd->qhk/dot_general | solution.py:30
  554.4 9.1 %fusion.80 = f32[512,16]{0,1:T(8,128)S(1)} fusion(f32[16,512,512]{2,1,0:T(8,128)} %get-tuple-element.311, f32[512,16]{0,1:T(8,128)S(1)} %max.22, f32[512,512]{0,1:T(8,128)S(1)} %bitcast.167), kind=kLoop, calls=%fused_computation.4.clone.1 | loop fusion | flops 16769024 | bytes 17891328 | tf_op jit(solution)/shard_map/while/body/eval_jaxpr/reduce_sum | solution.py:38
  563.5 9.9 %bitcast_add_fusion.5 = f32[512,16,64]{0,2,1:T(8,128)} fusion(f32[512,16,64]{0,2,1:T(8,128)} %get-tuple-element.362, bf16[512,16,64]{0,2,1:T(8,128)(2,1)S(1)} %bitcast.173, f32[16,512,512]{2,1,0:T(8,128)} %get-tuple-element.311, f32[512,16]{0,1:T(8,128)S(1)} %max.22, f32[512,512]{0,1:T(8,128)S(1)} %bitcast.168, f32[512,16]{0,1:T(8,128)S(1)} %get-tuple-element.314), kind=kOutput, calls=%fused_computation.7.clone.1 | convolution fusion | flops 554696704 | bytes 23134208 | tf_op jit(solution)/shard_map/while/body/eval_jaxpr/qhk,khd->qhd/dot_general | solution.py:39
  582.4 7.0 %fusion.79 = (f32[512,16]{0,1:T(8,128)S(1)}, f32[16,512,512]{2,1,0:T(8,128)}) fusion(f32[512,512]{0,1:T(8,128)S(1)} %bitcast.166, bf16[512,16,64]{0,2,1:T(8,128)(2,1)S(1)} %bitcast.175, bf16[512,16,64]{0,2,1:T(8,128)(2,1)S(1)} %get-tuple-element.372), kind=kOutput, calls=%fused_computation.5.clone.1 | convolution fusion | flops 549445632 | bytes 19955712 | tf_op jit(solution)/shard_map/while/body/eval_jaxpr/qhd,khd->qhk/dot_general | solution.py:30
  589.5 9.1 %fusion.80 = f32[512,16]{0,1:T(8,128)S(1)} fusion(f32[16,512,512]{2,1,0:T(8,128)} %get-tuple-element.311, f32[512,16]{0,1:T(8,128)S(1)} %max.22, f32[512,512]{0,1:T(8,128)S(1)} %bitcast.167), kind=kLoop, calls=%fused_computation.4.clone.1 | loop fusion | flops 16769024 | bytes 17891328 | tf_op jit(solution)/shard_map/while/body/eval_jaxpr/reduce_sum | solution.py:38
  598.6 9.9 %bitcast_add_fusion.5 = f32[512,16,64]{0,2,1:T(8,128)} fusion(f32[512,16,64]{0,2,1:T(8,128)} %get-tuple-element.362, bf16[512,16,64]{0,2,1:T(8,128)(2,1)S(1)} %bitcast.173, f32[16,512,512]{2,1,0:T(8,128)} %get-tuple-element.311, f32[512,16]{0,1:T(8,128)S(1)} %max.22, f32[512,512]{0,1:T(8,128)S(1)} %bitcast.168, f32[512,16]{0,1:T(8,128)S(1)} %get-tuple-element.314), kind=kOutput, calls=%fused_computation.7.clone.1 | convolution fusion | flops 554696704 | bytes 23134208 | tf_op jit(solution)/shard_map/while/body/eval_jaxpr/qhk,khd->qhd/dot_general | solution.py:39
  617.5 7.0 %fusion.79 = (f32[512,16]{0,1:T(8,128)S(1)}, f32[16,512,512]{2,1,0:T(8,128)}) fusion(f32[512,512]{0,1:T(8,128)S(1)} %bitcast.166, bf16[512,16,64]{0,2,1:T(8,128)(2,1)S(1)} %bitcast.175, bf16[512,16,64]{0,2,1:T(8,128)(2,1)S(1)} %get-tuple-element.372), kind=kOutput, calls=%fused_computation.5.clone.1 | convolution fusion | flops 549445632 | bytes 19955712 | tf_op jit(solution)/shard_map/while/body/eval_jaxpr/qhd,khd->qhk/dot_general | solution.py:30
  624.6 9.1 %fusion.80 = f32[512,16]{0,1:T(8,128)S(1)} fusion(f32[16,512,512]{2,1,0:T(8,128)} %get-tuple-element.311, f32[512,16]{0,1:T(8,128)S(1)} %max.22, f32[512,512]{0,1:T(8,128)S(1)} %bitcast.167), kind=kLoop, calls=%fused_computation.4.clone.1 | loop fusion | flops 16769024 | bytes 17891328 | tf_op jit(solution)/shard_map/while/body/eval_jaxpr/reduce_sum | solution.py:38
  633.7 9.9 %bitcast_add_fusion.5 = f32[512,16,64]{0,2,1:T(8,128)} fusion(f32[512,16,64]{0,2,1:T(8,128)} %get-tuple-element.362, bf16[512,16,64]{0,2,1:T(8,128)(2,1)S(1)} %bitcast.173, f32[16,512,512]{2,1,0:T(8,128)} %get-tuple-element.311, f32[512,16]{0,1:T(8,128)S(1)} %max.22, f32[512,512]{0,1:T(8,128)S(1)} %bitcast.168, f32[512,16]{0,1:T(8,128)S(1)} %get-tuple-element.314), kind=kOutput, calls=%fused_computation.7.clone.1 | convolution fusion | flops 554696704 | bytes 23134208 | tf_op jit(solution)/shard_map/while/body/eval_jaxpr/qhk,khd->qhd/dot_general | solution.py:39
  652.6 7.0 %fusion.79 = (f32[512,16]{0,1:T(8,128)S(1)}, f32[16,512,512]{2,1,0:T(8,128)}) fusion(f32[512,512]{0,1:T(8,128)S(1)} %bitcast.166, bf16[512,16,64]{0,2,1:T(8,128)(2,1)S(1)} %bitcast.175, bf16[512,16,64]{0,2,1:T(8,128)(2,1)S(1)} %get-tuple-element.372), kind=kOutput, calls=%fused_computation.5.clone.1 | convolution fusion | flops 549445632 | bytes 19955712 | tf_op jit(solution)/shard_map/while/body/eval_jaxpr/qhd,khd->qhk/dot_general | solution.py:30
  659.7 9.1 %fusion.80 = f32[512,16]{0,1:T(8,128)S(1)} fusion(f32[16,512,512]{2,1,0:T(8,128)} %get-tuple-element.311, f32[512,16]{0,1:T(8,128)S(1)} %max.22, f32[512,512]{0,1:T(8,128)S(1)} %bitcast.167), kind=kLoop, calls=%fused_computation.4.clone.1 | loop fusion | flops 16769024 | bytes 17891328 | tf_op jit(solution)/shard_map/while/body/eval_jaxpr/reduce_sum | solution.py:38
  668.8 9.9 %bitcast_add_fusion.5 = f32[512,16,64]{0,2,1:T(8,128)} fusion(f32[512,16,64]{0,2,1:T(8,128)} %get-tuple-element.362, bf16[512,16,64]{0,2,1:T(8,128)(2,1)S(1)} %bitcast.173, f32[16,512,512]{2,1,0:T(8,128)} %get-tuple-element.311, f32[512,16]{0,1:T(8,128)S(1)} %max.22, f32[512,512]{0,1:T(8,128)S(1)} %bitcast.168, f32[512,16]{0,1:T(8,128)S(1)} %get-tuple-element.314), kind=kOutput, calls=%fused_computation.7.clone.1 | convolution fusion | flops 554696704 | bytes 23134208 | tf_op jit(solution)/shard_map/while/body/eval_jaxpr/qhk,khd->qhd/dot_general | solution.py:39
  (168 shorter events, 121.4 us)
Async XLA Ops:
  6.5 2.2 copy-start
  6.5 83.6 %all-gather.2.cloned.1.call-start = ((), (), s32[]{:S(2)}) async-start(), calls=%async_computation.2 | async-start | bytes 8454144 | tf_op jit(solution)/shard_map/all_gather | solution.py:81
  10.6 2.7 copy-start.2
  10.6 2.7 copy-start.4
  13.3 8.8 %copy-start.3 = (s32[1,4,8,2]{2,3,1,0:T(2,128)S(1)}, s32[1,4,8,2]{2,3,1,0:T(2,128)}, u32[]{:S(2)}) copy-start(s32[1,4,8,2]{2,3,1,0:T(2,128)} %param.17) | copy-start | bytes 772
  16.1 29.1 %collective-permute-start.1 = (bf16[512,2,1024]{2,0,1:T(8,128)(2,1)}, bf16[512,2,1024]{2,0,1:T(8,128)(2,1)}, u32[]{:S(2)}, u32[]{:S(2)}) collective-permute-start(bf16[512,2,1024]{2,0,1:T(8,128)(2,1)} %pad_maximum_fusion.1), channel_id=1, source_target_pairs={{1,0},{2,1},{3,2},{4,3},{5,4},{6,5},{7,6},{9,8},{10,9},{11,10},{12... | collective-permute-start | bytes 6291464 | tf_op jit(solution)/shard_map/ppermute | solution.py:19
  18.6 28.3 %collective-permute-start = (bf16[512,2,1024]{2,0,1:T(8,128)(2,1)}, bf16[512,2,1024]{2,0,1:T(8,128)(2,1)}, u32[]{:S(2)}, u32[]{:S(2)}) collective-permute-start(bf16[512,2,1024]{2,0,1:T(8,128)(2,1)} %pad_maximum_fusion.1), channel_id=1, source_target_pairs={{0,1},{1,2},{2,3},{3,4},{4,5},{5,6},{6,7},{8,9},{9,10},{10,11},{11... | collective-permute-start | bytes 6291464 | tf_op jit(solution)/shard_map/ppermute | solution.py:18
  78.8 7.9 %copy-start.5 = (bf16[1,512,1024]{2,1,0:T(8,128)(2,1)S(1)}, bf16[1,512,1024]{2,1,0:T(8,128)(2,1)}, u32[]{:S(2)}) copy-start(bf16[1,512,1024]{2,1,0:T(8,128)(2,1)} %param.11) | copy-start | bytes 3145732
  78.8 305.3 %all-to-all-start.1 = ((bf16[16,2,128,2,1024]{4,2,1,3,0:T(8,128)(2,1)}), bf16[16,2,128,2,1024]{4,2,1,3,0:T(8,128)(2,1)}, u32[]{:S(2)}, u32[]{:S(2)}) async-start(bf16[16,2,128,2,1024]{4,2,1,3,0:T(8,128)(2,1)} %copy.99), calls=%async_computation.1 | async-start | bytes 33554432 | tf_op jit(solution)/shard_map/all_to_all | solution.py:108
  678.6 5.9 copy-start.1
Sparse Core Ops, SparseCore 0:
  10.7 71.3 all-gather.1
where the time goes:
time: 696 us; the launch traced here: 691 us
  matrix products  225 us (32%)
  waiting for transfers between devices  170 us (24%)
  local copies, waits for them, and re-layouts  129 us (19%)
  other arithmetic  127 us (18%)
  between operations  13.6 us (2%)
  starting transfers between devices  13.4 us (2%)
  blocking collectives  13 us (2%)
    all_to_all x1, waiting for transfers between devices, local(): lax.all_to_all(wanted, 'view', split_axis=0, concat_axis=0, tiled=True)  160 us
    dot_general x12, matrix products, attend(): jnp.einsum('qhk,khd->qhd', weights.astype(jnp.bfloat16), value_heads, pre...  122 us
    reduce_sum x12, other arithmetic, attend(): total = total * factor + jnp.sum(weights, axis=-1)  107 us
    dot_general x12, matrix products, attend(): jnp.einsum('qhd,khd->qhk', query_heads, key_heads, preferred_element_type...  88.7 us
    dynamic_slice x16, local copies, waits for them, and re-layouts, local(): carry, _ = lax.scan(body_step, carry, (key_groups, mask_groups))  56.5 us
    dynamic_slice x8, local copies, waits for them, and re-layouts, attend_panel(): carry, _ = lax.scan(attend_step, carry, blocks)  23.7 us
  transfers between devices with their start and end apart: 4, of which 3 were waited for; matrix products, arithmetic and copies ran while one was open for 25% of the time, Pallas kernels for 0%

commit v1 on v0

v1 whole, which is shorter than its diff:
```python
import functools
import math

import jax
import jax.numpy as jnp
from jax import lax
from jax.experimental import pallas as pl
from jax.experimental.pallas import tpu as pltpu
from jax.sharding import PartitionSpec as P

HD = 64
BLK = 128
MESH = pl.DeviceIdType.MESH
LAG = 3


def dot(a, b):
    return jnp.dot(a, b, preferred_element_type=jnp.float32)


def dot_t(a, b):
    return lax.dot_general(a, b, (((1,), (1,)), ((), ())), preferred_element_type=jnp.float32)


def kernel(
    nview, ntok, rows, crows, most,
    x_hbm, cond_hbm, wq_hbm, wk_hbm, wv_hbm, wo_hbm, lists_hbm,
    out_hbm,
    xall, wq, wk, wv, wo,
    qsend, kvsend, csend, lsend,
    qrecv, pool, condkv, lists_v, lists_s,
    vcond, qpad, oacc, mrow, osend, orecv, att, outv,
    load_sem, q_ss, q_rs, kv_ss, kv_rs, c_ss, c_rs, l_ss, l_rs, g_ss, g_rs, f_ss, f_rs, o_ss, o_rs, smem_sem, out_sem,
):
    view = lax.axis_index("view")
    tok = lax.axis_index("tok")
    width = nview * HD
    half = rows // 2
    nblk = rows // BLK
    scale = math.log2(math.e) * HD ** -0.5

    loads = [
        pltpu.make_async_copy(cond_hbm, xall.at[pl.ds(rows, crows)], load_sem.at[0]),
        pltpu.make_async_copy(x_hbm, xall.at[pl.ds(0, rows)], load_sem.at[1]),
        pltpu.make_async_copy(wk_hbm, wk, load_sem.at[2]),
        pltpu.make_async_copy(wv_hbm, wv, load_sem.at[3]),
        pltpu.make_async_copy(lists_hbm, lsend, load_sem.at[4]),
        pltpu.make_async_copy(wq_hbm, wq, load_sem.at[5]),
        pltpu.make_async_copy(wo_hbm, wo, load_sem.at[6]),
    ]
    for load in loads:
        load.start()

    barrier = pltpu.get_barrier_semaphore()

    def greet_view(i, c):
        pl.semaphore_signal(
            barrier, inc=1, device_id=(lax.rem(view + i, nview), tok), device_id_type=MESH
        )
        return c

    def greet_tok(i, c):
        pl.semaphore_signal(
            barrier, inc=1, device_id=(view, lax.rem(tok + i, ntok)), device_id_type=MESH
        )
        return c

    lax.fori_loop(1, nview, greet_view, 0)
    lax.fori_loop(1, ntok, greet_tok, 0)

    low = lax.broadcasted_iota(jnp.int32, (1, 2 * HD), 1) < HD

    for load in loads[:5]:
        load.wait()

    def project_kv(j, c):
        columns = pl.ds(pl.multiple_of(j * 256, 256), 256)
        keys = dot(xall[...], wk[:, columns])
        values = dot(xall[...], wv[:, columns])
        for p in range(2):
            k = keys[:, p * 128 : (p + 1) * 128]
            v = pltpu.roll(values[:, p * 128 : (p + 1) * 128], HD, 1)
            even = jnp.where(low, k, v).astype(jnp.bfloat16)
            odd = jnp.where(low, v, k).astype(jnp.bfloat16)
            kvsend[4 * j + 2 * p] = even[:rows].reshape(nblk, BLK, 2 * HD)
            kvsend[4 * j + 2 * p + 1] = odd[:rows].reshape(nblk, BLK, 2 * HD)
            csend[4 * j + 2 * p] = even[rows:]
            csend[4 * j + 2 * p + 1] = odd[rows:]
        return c

    lax.fori_loop(0, width // 256, project_kv, 0)

    pl.semaphore_wait(barrier, nview + ntok - 2)

    def view_copy(i, name):
        to = lax.rem(view + i, nview)
        target = (to, tok)

        def remote(src, dst, send, recv):
            return pltpu.make_async_remote_copy(
                src_ref=src, dst_ref=dst, send_sem=send.at[i], recv_sem=recv.at[i],
                device_id=target, device_id_type=MESH,
            )

        if name == "c":
            return remote(csend.at[to], condkv.at[tok, view], c_ss, c_rs)
        if name == "l":
            return remote(lsend, lists_v.at[view], l_ss, l_rs)
        if name == "q":
            return remote(qsend.at[to], qrecv.at[view], q_ss, q_rs)
        own = pool.at[pl.ds((nview + view) * nblk, nblk)]
        return remote(kvsend.at[to], own, kv_ss, kv_rs)

    def start(*names):
        def body(i, c):
            for name in names:
                view_copy(i, name).start()
            return c

        lax.fori_loop(1, nview, body, 0)

    start("c", "l")
    condkv[tok, view] = csend[view]
    lists_v[view] = lsend[...]

    loads[5].wait()

    def project_q(j, c):
        columns = pl.ds(pl.multiple_of(j * 256, 256), 256)
        query = dot(xall[pl.ds(0, rows), :], wq[:, columns])
        for p in range(2):
            first = query[:half, p * 128 : (p + 1) * 128]
            second = pltpu.roll(query[half:, p * 128 : (p + 1) * 128], HD, 1)
            qsend[4 * j + 2 * p] = jnp.where(low, first, second).astype(jnp.bfloat16)
            qsend[4 * j + 2 * p + 1] = jnp.where(low, second, first).astype(jnp.bfloat16)
        return c

    lax.fori_loop(0, width // 256, project_q, 0)
    start("q")
    start("kv")
    qrecv[view] = qsend[view]
    pool[pl.ds((nview + view) * nblk, nblk)] = kvsend[view]

    def wait_view(name, start_i=1):
        def body(i, c):
            view_copy(i, name).wait_recv()
            return c

        lax.fori_loop(start_i, nview, body, 0)

    wait_view("c")

    def tok_copy(i):
        return pltpu.make_async_remote_copy(
            src_ref=condkv.at[tok], dst_ref=condkv.at[tok],
            send_sem=g_ss.at[i], recv_sem=g_rs.at[i],
            device_id=(view, lax.rem(tok + i, ntok)), device_id_type=MESH,
        )

    def start_tok(i, c):
        tok_copy(i).start()
        return c

    def wait_tok(i, c):
        tok_copy(i).wait_recv()
        return c

    lax.fori_loop(1, ntok, start_tok, 0)
    lax.fori_loop(1, ntok, wait_tok, 0)

    parity = lax.rem(view, 2)
    lane = lax.broadcasted_iota(jnp.int32, (1, 2 * HD), 1)
    khalf = (lane // HD) == parity
    kf = jnp.where(khalf, 1.0, 0.0)
    krow = kf.astype(jnp.bfloat16)
    vrow = (1.0 - kf).astype(jnp.bfloat16)
    count = ntok * nview * crows

    pool[3 * nview * nblk] = condkv[0, pl.ds(0, BLK // crows)].reshape(BLK, 2 * HD)
    vcond[...] = condkv[...].reshape(count, 2 * HD) * vrow + krow

    def forward(i, direction):
        at = pl.ds((nview + lax.rem(view - i + nview, nview)) * nblk, nblk)
        to = pl.ds((2 * direction * nview + lax.rem(view - i + nview, nview)) * nblk, nblk)
        step = 1 if direction == 0 else ntok - 1
        return pltpu.make_async_remote_copy(
            src_ref=pool.at[at], dst_ref=pool.at[to],
            send_sem=f_ss.at[direction, i], recv_sem=f_rs.at[direction, i],
            device_id=(view, lax.rem(tok + step, ntok)), device_id_type=MESH,
        )

    forward(0, 0).start()
    forward(0, 1).start()

    def pass_on(i):
        view_copy(i, "kv").wait_recv()
        forward(i, 0).start()
        forward(i, 1).start()

    def cond_step(i, c):
        @pl.when(i > 0)
        def _():
            view_copy(i, "q").wait_recv()

        owner = lax.rem(view - i + nview, nview)
        packed = qrecv[owner].astype(jnp.float32)
        qpad[i, pl.ds(0, half)] = jnp.where(khalf, packed, 0.0).astype(jnp.bfloat16)
        qpad[i, pl.ds(half, half)] = jnp.where(khalf, pltpu.roll(packed, HD, 1), 0.0).astype(
            jnp.bfloat16
        )
        ck = condkv[...].reshape(count, 2 * HD)
        for part in range(2):
            at = pl.ds(part * half, half)
            scores = dot_t(qpad[i, at], ck)
            peak = jnp.max(scores, axis=1, keepdims=True)
            weights = jnp.exp2((scores - peak) * scale).astype(jnp.bfloat16)
            oacc[i, at] = dot(weights, vcond[...])
            mrow[i, at] = jnp.broadcast_to(peak, (half, 2 * HD))

        @pl.when(i > LAG)
        def _():
            pass_on(i - LAG)

        return c

    lax.fori_loop(0, nview, cond_step, 0)

    def rest(i, c):
        pass_on(i)
        return c

    lax.fori_loop(nview - LAG, nview, rest, 0)
    wait_view("l")
    to_smem = pltpu.make_async_copy(lists_v, lists_s, smem_sem)
    to_smem.start()
    to_smem.wait()

    def wait_forward(i, c):
        forward(i, 0).wait_recv()
        forward(i, 1).wait_recv()
        return c

    lax.fori_loop(0, nview, wait_forward, 0)

    def o_copy(i):
        return pltpu.make_async_remote_copy(
            src_ref=osend.at[i], dst_ref=orecv.at[view],
            send_sem=o_ss.at[i], recv_sem=o_rs.at[i],
            device_id=(lax.rem(view - i + nview, nview), tok), device_id_type=MESH,
        )

    def epi_step(i, c):
        owner = lax.rem(view - i + nview, nview)
        parts = []
        for b in range(nblk):
            at = pl.ds(b * BLK, BLK)
            kvs, vvs = [], []
            for s in range(most):
                entry = lists_s[owner, 0, b * most + s]
                used = jnp.where(entry < 3 * nview * nblk, 1.0, 0.0)
                block = pool[entry]
                kvs.append(block)
                vvs.append(
                    block * ((1.0 - kf) * used).astype(jnp.bfloat16)
                    + (kf * used).astype(jnp.bfloat16)
                )
            scores = dot_t(qpad[i, at], jnp.concatenate(kvs, axis=0))
            before = mrow[i, at]
            peak = jnp.maximum(before[:, :1], jnp.max(scores, axis=1, keepdims=True))
            weights = jnp.exp2((scores - peak) * scale).astype(jnp.bfloat16)
            total = oacc[i, at] * jnp.exp2((before - peak) * scale) + dot(
                weights, jnp.concatenate(vvs, axis=0)
            )
            parts.append(total / pltpu.roll(total, HD, 1))
        first = jnp.concatenate(parts[: nblk // 2], axis=0)
        second = pltpu.roll(jnp.concatenate(parts[nblk // 2 :], axis=0), HD, 1)
        osend[i] = jnp.where(khalf, second, first).astype(jnp.bfloat16)

        @pl.when(i > 0)
        def _():
            o_copy(i).start()

        @pl.when(i == 0)
        def _():
            orecv[view] = osend[i]

        return c

    lax.fori_loop(0, nview, epi_step, 0)

    loads[6].wait()

    def wait_o(i, c):
        o_copy(i).wait_recv()
        return c

    lax.fori_loop(1, nview, wait_o, 0)

    for j in range(nview // 2):
        even = orecv[2 * j].astype(jnp.float32)
        odd = orecv[2 * j + 1].astype(jnp.float32)
        at = pl.ds(j * 128, 128)
        att[pl.ds(0, half), at] = pltpu.roll(jnp.where(low, odd, even), HD, 1).astype(jnp.bfloat16)
        att[pl.ds(half, half), at] = jnp.where(low, even, odd).astype(jnp.bfloat16)

    def project_out(j, c):
        columns = pl.ds(pl.multiple_of(j * 256, 256), 256)
        outv[:, columns] = dot(att[...], wo[:, columns]).astype(jnp.bfloat16)
        return c

    lax.fori_loop(0, width // 256, project_out, 0)
    store = pltpu.make_async_copy(outv, out_hbm, out_sem)
    store.start()

    def wait_sends(i, c):
        for name in ("c", "l", "q", "kv"):
            view_copy(i, name).wait_send()
        o_copy(i).wait_send()
        return c

    def wait_tok_sends(i, c):
        tok_copy(i).wait_send()
        return c

    def wait_forward_sends(i, c):
        forward(i, 0).wait_send()
        forward(i, 1).wait_send()
        return c

    lax.fori_loop(1, nview, wait_sends, 0)
    lax.fori_loop(1, ntok, wait_tok_sends, 0)
    lax.fori_loop(0, nview, wait_forward_sends, 0)
    store.wait()


def local(x_target, cond_x, w_query, w_key, w_value, w_out, epi_lists):
    nview = lax.axis_size("view")
    ntok = lax.axis_size("tok")
    rows, width = x_target.shape[1:]
    crows = cond_x.shape[0]
    most = epi_lists.shape[2]
    nblk = rows // BLK
    band = lax.axis_index("tok")
    entry_view = epi_lists[0, :, :, 0].reshape(-1)
    entry_block = epi_lists[0, :, :, 1].reshape(-1) - (band - 1) * nblk
    place = ((entry_block // nblk) * nview + entry_view) * nblk + entry_block % nblk
    place = jnp.where(entry_view >= 0, place, 3 * nview * nblk)
    lists = jnp.zeros((8, 128), jnp.int32).at[0, : nblk * most].set(place)
    bf, f32 = jnp.bfloat16, jnp.float32
    half = rows // 2
    dma = pltpu.SemaphoreType.DMA
    scratch = [
        pltpu.VMEM((rows + crows, width), bf),
        pltpu.VMEM((width, width), bf),
        pltpu.VMEM((width, width), bf),
        pltpu.VMEM((width, width), bf),
        pltpu.VMEM((width, width), bf),
        pltpu.VMEM((nview, half, 128), bf),
        pltpu.VMEM((nview, nblk, BLK, 128), bf),
        pltpu.VMEM((nview, crows, 128), bf),
        pltpu.VMEM((8, 128), jnp.int32),
        pltpu.VMEM((nview, half, 128), bf),
        pltpu.VMEM((3 * nview * nblk + 1, BLK, 128), bf),
        pltpu.VMEM((ntok, nview, crows, 128), bf),
        pltpu.VMEM((nview, 8, 128), jnp.int32),
        pltpu.SMEM((nview, 8, 128), jnp.int32),
        pltpu.VMEM((ntok * nview * crows, 128), bf),
        pltpu.VMEM((nview, rows, 128), bf),
        pltpu.VMEM((nview, rows, 128), f32),
        pltpu.VMEM((nview, rows, 128), f32),
        pltpu.VMEM((nview, half, 128), bf),
        pltpu.VMEM((nview, half, 128), bf),
        pltpu.VMEM((rows, width), bf),
        pltpu.VMEM((rows, width), bf),
        dma((7,)),
        *[dma((nview,)) for _ in range(8)],
        dma((ntok,)), dma((ntok,)),
        dma((2, nview)), dma((2, nview)),
        dma((nview,)), dma((nview,)),
        dma, dma,
    ]
    mixed = pl.pallas_call(
        functools.partial(kernel, nview, ntok, rows, crows, most),
        out_shape=jax.ShapeDtypeStruct((rows, width), bf),
        in_specs=[pl.BlockSpec(memory_space=pl.ANY)] * 7,
        out_specs=pl.BlockSpec(memory_space=pl.ANY),
        scratch_shapes=scratch,
        compiler_params=pltpu.CompilerParams(
            collective_id=0, has_side_effects=True, vmem_limit_bytes=60 * 1024 * 1024
        ),
    )(x_target[0], cond_x, w_query, w_key, w_value, w_out, lists)
    return mixed[None]


def solution(mesh):
    placed = (
        P("view", "tok", None),
        P(("view", "tok"), None),
        P(),
        P(),
        P(),
        P(),
        P("view", "tok", None, None),
    )
    return jax.shard_map(
        local, mesh=mesh, in_specs=placed, out_specs=P("view", "tok", None), check_vma=False
    )
```

time: 696 us -> 125 us (0.18)
  matrix products: 225 us -> 0 us
  waiting for transfers between devices: 170 us -> 0 us
  other arithmetic: 127 us -> 0.8 us
  local copies, waits for them, and re-layouts: 129 us -> 3.03 us
  Pallas kernels: 0 us -> 119 us
  between operations: 13.6 us -> 0.01 us
  starting transfers between devices: 13.4 us -> 0 us
  blocking collectives: 13 us -> 0 us
    dot_general x32 -> x0, matrix products: 225 us -> none  [the longest x12 122 us: attend(): jnp.einsum('qhk,khd->qhd', weights.astype(jnp.bfloat16), value_heads, pre...]
    all_to_all x1 -> x0, waiting for transfers between devices: 160 us -> none  [local(): lax.all_to_all(wanted, 'view', split_axis=0, concat_axis=0, tiled=True)]
    pallas_call x0 -> x1, Pallas kernels: none -> 119 us  [local(): pl.pallas_call(functools.partial(kernel, nview, ntok, rows, crows, most),...]
    reduce_sum x13 -> x0, other arithmetic: 107 us -> none  [the longest x12 107 us: attend(): total = total * factor + jnp.sum(weights, axis=-1)]
    dynamic_slice x24 -> x0, local copies, waits for them, and re-layouts: 80.3 us -> none  [the longest x16 56.5 us: local(): carry, _ = lax.scan(body_step, carry, (key_groups, mask_groups))]
    slice x12 -> x0, local copies, waits for them, and re-layouts: 14 us -> none  [the longest x8 13.4 us: body_step(): return (attend(state, query_heads, piece[:, 0], piece[:, 1], bias), None)]
    all_to_all x2 -> x0, local copies, waits for them, and re-layouts: 13.9 us -> none  [the longest x1 13.9 us: local(): lax.all_to_all(wanted, 'view', split_axis=0, concat_axis=0, tiled=True)]
    all_to_all x1 -> x0, blocking collectives: 13 us -> none  [local(): lax.all_to_all(request, 'view', split_axis=0, concat_axis=0, tiled=True)]
  transfers between devices with their start and end apart: 4 -> 0, of which waited for: 3 -> 0; matrix products, arithmetic and copies ran while one was open for 25% -> 0% of each run, Pallas kernels for 0% -> 0%
where the time goes in v1:
time: 125 us; the launch traced here: 123 us
  Pallas kernels  119 us (95%)
  local copies, waits for them, and re-layouts  3.03 us (2%)
    pallas_call x1, Pallas kernels, local(): pl.pallas_call(functools.partial(kernel, nview, ntok, rows, crows, most),...  119 us

profile of v1, /device:TPU:33, one launch (start us, length us, event | category | flops | bytes accessed | tf_op | source)
XLA Modules:
  0.0 123.1 jit_solution(9744432142937201259)
XLA Ops:
  0.0 0.8 subtract_reduce_fusion
  0.8 0.1 sub.26
  0.9 0.1 reshape_squeeze.4
  1.0 0.6 scatter.4.lists_hbm
  1.6 119.2 %shard_map.73 = bf16[512,1024]{1,0:T(8,128)(2,1)} custom-call(bf16[512,1024]{1,0:T(8,128)(2,1)} %bitcast.3, bf16[16,1024]{1,0:T(8,128)(2,1)} %cond_hbm.1, bf16[1024,1024]{1,0:T(8,128)(2,1)} %wq_hbm.1, bf16[1024,1024]{1,0:T(8,128)(2,1)} %wk_hbm.1, bf16[1024,1024]{1,0:T(8,128)(2,1)} %wv_hbm.1, bf16[1024,1024]{1,0:T(8,128)(2,1)} %wo_hbm.1, ...), custom_call_target="tpu_custom_call" | custom-call | tf_op jit(solution)/shard_map/pallas_call | solution.py:382
  120.8 2.3 %copy.9 = bf16[1,512,1024]{2,1,0:T(8,128)(2,1)} copy(bf16[1,512,1024]{2,1,0:T(8,128)(2,1)} %bitcast.2) | data formatting | bytes 2097152
  (1 shorter events, 0.0 us)

commit v2 on v1

--- a/solution.py
+++ b/solution.py
@@ -11,7 +11,8 @@
 HD = 64
 BLK = 128
 MESH = pl.DeviceIdType.MESH
-LAG = 3
+LAG = 2
+CHUNKS = 1
 
 
 def dot(a, b):
@@ -23,13 +24,13 @@
 
 
 def kernel(
-    nview, ntok, rows, crows, most,
-    x_hbm, cond_hbm, wq_hbm, wk_hbm, wv_hbm, wo_hbm, lists_hbm,
+    nview, ntok, side, rows, crows, most,
+    x_hbm, cond_hbm, wq_hbm, wk_hbm, wv_hbm, lists_hbm,
     out_hbm,
-    xall, wq, wk, wv, wo,
+    xall, wq, wk, wv,
     qsend, kvsend, csend, lsend,
     qrecv, pool, condkv, lists_v, lists_s,
-    vcond, qpad, oacc, mrow, osend, orecv, att, outv,
+    vcond, qpad, oacc, mrow, osend, orecv, att,
     load_sem, q_ss, q_rs, kv_ss, kv_rs, c_ss, c_rs, l_ss, l_rs, g_ss, g_rs, f_ss, f_rs, o_ss, o_rs, smem_sem, out_sem,
 ):
     view = lax.axis_index("view")
@@ -46,17 +47,20 @@
         pltpu.make_async_copy(wv_hbm, wv, load_sem.at[3]),
         pltpu.make_async_copy(lists_hbm, lsend, load_sem.at[4]),
         pltpu.make_async_copy(wq_hbm, wq, load_sem.at[5]),
-        pltpu.make_async_copy(wo_hbm, wo, load_sem.at[6]),
     ]
     for load in loads:
         load.start()
 
     barrier = pltpu.get_barrier_semaphore()
 
+    def peer(i, sign):
+        dx, dy = lax.rem(i, side), lax.rem(i + i // side, side)
+        x = lax.rem(view // side + sign * dx + side, side)
+        y = lax.rem(lax.rem(view, side) + sign * dy + side, side)
+        return x * side + y
+
     def greet_view(i, c):
-        pl.semaphore_signal(
-            barrier, inc=1, device_id=(lax.rem(view + i, nview), tok), device_id_type=MESH
-        )
+        pl.semaphore_signal(barrier, inc=1, device_id=(peer(i, 1), tok), device_id_type=MESH)
         return c
 
     def greet_tok(i, c):
@@ -92,13 +96,16 @@
 
     pl.semaphore_wait(barrier, nview + ntok - 2)
 
-    def view_copy(i, name):
-        to = lax.rem(view + i, nview)
+    piece = nblk // CHUNKS
+
+    def view_copy(i, name, part=0):
+        to = peer(i, 1)
         target = (to, tok)
 
         def remote(src, dst, send, recv):
+            at = part * nview + i
             return pltpu.make_async_remote_copy(
-                src_ref=src, dst_ref=dst, send_sem=send.at[i], recv_sem=recv.at[i],
+                src_ref=src, dst_ref=dst, send_sem=send.at[at], recv_sem=recv.at[at],
                 device_id=target, device_id_type=MESH,
             )
 
@@ -108,13 +115,13 @@
             return remote(lsend, lists_v.at[view], l_ss, l_rs)
         if name == "q":
             return remote(qsend.at[to], qrecv.at[view], q_ss, q_rs)
-        own = pool.at[pl.ds((nview + view) * nblk, nblk)]
-        return remote(kvsend.at[to], own, kv_ss, kv_rs)
-
-    def start(*names):
+        own = pool.at[pl.ds((nview + view) * nblk + part * piece, piece)]
+        return remote(kvsend.at[to, pl.ds(part * piece, piece)], own, kv_ss, kv_rs)
+
+    def start(*names, part=0):
         def body(i, c):
             for name in names:
-                view_copy(i, name).start()
+                view_copy(i, name, part).start()
             return c
 
         lax.fori_loop(1, nview, body, 0)
@@ -137,7 +144,8 @@
 
     lax.fori_loop(0, width // 256, project_q, 0)
     start("q")
-    start("kv")
+    for part in range(CHUNKS):
+        start("kv", part=part)
     qrecv[view] = qsend[view]
     pool[pl.ds((nview + view) * nblk, nblk)] = kvsend[view]
 
@@ -179,47 +187,52 @@
     pool[3 * nview * nblk] = condkv[0, pl.ds(0, BLK // crows)].reshape(BLK, 2 * HD)
     vcond[...] = condkv[...].reshape(count, 2 * HD) * vrow + krow
 
-    def forward(i, direction):
-        at = pl.ds((nview + lax.rem(view - i + nview, nview)) * nblk, nblk)
-        to = pl.ds((2 * direction * nview + lax.rem(view - i + nview, nview)) * nblk, nblk)
+    def forward(i, part, direction):
+        owner = peer(i, -1) * nblk + part * piece
+        at = pl.ds(nview * nblk + owner, piece)
+        to = pl.ds(2 * direction * nview * nblk + owner, piece)
         step = 1 if direction == 0 else ntok - 1
+        sem = part * nview + i
         return pltpu.make_async_remote_copy(
             src_ref=pool.at[at], dst_ref=pool.at[to],
-            send_sem=f_ss.at[direction, i], recv_sem=f_rs.at[direction, i],
+            send_sem=f_ss.at[direction, sem], recv_sem=f_rs.at[direction, sem],
             device_id=(view, lax.rem(tok + step, ntok)), device_id_type=MESH,
         )
 
-    forward(0, 0).start()
-    forward(0, 1).start()
-
-    def pass_on(i):
-        view_copy(i, "kv").wait_recv()
-        forward(i, 0).start()
-        forward(i, 1).start()
+    for part in range(CHUNKS):
+        forward(0, part, 0).start()
+        forward(0, part, 1).start()
+
+    units = CHUNKS * (nview - 1)
+
+    def pass_on(u):
+        part, i = u // (nview - 1), 1 + lax.rem(u, nview - 1)
+        view_copy(i, "kv", part).wait_recv()
+        forward(i, part, 0).start()
+        forward(i, part, 1).start()
 
     def cond_step(i, c):
         @pl.when(i > 0)
         def _():
             view_copy(i, "q").wait_recv()
 
-        owner = lax.rem(view - i + nview, nview)
-        packed = qrecv[owner].astype(jnp.float32)
+        packed = qrecv[peer(i, -1)].astype(jnp.float32)
         qpad[i, pl.ds(0, half)] = jnp.where(khalf, packed, 0.0).astype(jnp.bfloat16)
         qpad[i, pl.ds(half, half)] = jnp.where(khalf, pltpu.roll(packed, HD, 1), 0.0).astype(
             jnp.bfloat16
         )
         ck = condkv[...].reshape(count, 2 * HD)
+        scores = [dot_t(qpad[i, pl.ds(part * half, half)], ck) for part in range(2)]
         for part in range(2):
             at = pl.ds(part * half, half)
-            scores = dot_t(qpad[i, at], ck)
-            peak = jnp.max(scores, axis=1, keepdims=True)
-            weights = jnp.exp2((scores - peak) * scale).astype(jnp.bfloat16)
+            peak = jnp.max(scores[part], axis=1, keepdims=True)
+            weights = jnp.exp2((scores[part] - peak) * scale).astype(jnp.bfloat16)
             oacc[i, at] = dot(weights, vcond[...])
             mrow[i, at] = jnp.broadcast_to(peak, (half, 2 * HD))
 
-        @pl.when(i > LAG)
+        @pl.when(i >= LAG)
         def _():
-            pass_on(i - LAG)
+            pass_on(CHUNKS * (i - LAG))
 
         return c
 
@@ -229,15 +242,16 @@
         pass_on(i)
         return c
 
-    lax.fori_loop(nview - LAG, nview, rest, 0)
+    lax.fori_loop(CHUNKS * (nview - LAG), units, rest, 0)
     wait_view("l")
     to_smem = pltpu.make_async_copy(lists_v, lists_s, smem_sem)
     to_smem.start()
     to_smem.wait()
 
     def wait_forward(i, c):
-        forward(i, 0).wait_recv()
-        forward(i, 1).wait_recv()
+        for part in range(CHUNKS):
+            forward(i, part, 0).wait_recv()
+            forward(i, part, 1).wait_recv()
         return c
 
     lax.fori_loop(0, nview, wait_forward, 0)
@@ -246,17 +260,17 @@
         return pltpu.make_async_remote_copy(
             src_ref=osend.at[i], dst_ref=orecv.at[view],
             send_sem=o_ss.at[i], recv_sem=o_rs.at[i],
-            device_id=(lax.rem(view - i + nview, nview), tok), device_id_type=MESH,
+            device_id=(peer(i, -1), tok), device_id_type=MESH,
         )
 
-    def epi_step(i, c):
-        owner = lax.rem(view - i + nview, nview)
-        parts = []
+    def epi_step(j, c):
+        i = lax.rem(j + 1, nview)
+        owner = peer(i, -1)
+        scores, values, parts = [], [], []
         for b in range(nblk):
-            at = pl.ds(b * BLK, BLK)
             kvs, vvs = [], []
             for s in range(most):
-                entry = lists_s[owner, 0, b * most + s]
+                entry = lists_s[owner, b, s]
                 used = jnp.where(entry < 3 * nview * nblk, 1.0, 0.0)
                 block = pool[entry]
                 kvs.append(block)
@@ -264,13 +278,14 @@
                     block * ((1.0 - kf) * used).astype(jnp.bfloat16)
                     + (kf * used).astype(jnp.bfloat16)
                 )
-            scores = dot_t(qpad[i, at], jnp.concatenate(kvs, axis=0))
+            scores.append(dot_t(qpad[i, pl.ds(b * BLK, BLK)], jnp.concatenate(kvs, axis=0)))
+            values.append(jnp.concatenate(vvs, axis=0))
+        for b in range(nblk):
+            at = pl.ds(b * BLK, BLK)
             before = mrow[i, at]
-            peak = jnp.maximum(before[:, :1], jnp.max(scores, axis=1, keepdims=True))
-            weights = jnp.exp2((scores - peak) * scale).astype(jnp.bfloat16)
-            total = oacc[i, at] * jnp.exp2((before - peak) * scale) + dot(
-                weights, jnp.concatenate(vvs, axis=0)
-            )
+            peak = jnp.maximum(before[:, :1], jnp.max(scores[b], axis=1, keepdims=True))
+            weights = jnp.exp2((scores[b] - peak) * scale).astype(jnp.bfloat16)
+            total = oacc[i, at] * jnp.exp2((before - peak) * scale) + dot(weights, values[b])
             parts.append(total / pltpu.roll(total, HD, 1))
         first = jnp.concatenate(parts[: nblk // 2], axis=0)
         second = pltpu.roll(jnp.concatenate(parts[nblk // 2 :], axis=0), HD, 1)
@@ -287,8 +302,6 @@
         return c
 
     lax.fori_loop(0, nview, epi_step, 0)
-
-    loads[6].wait()
 
     def wait_o(i, c):
         o_copy(i).wait_recv()
@@ -303,18 +316,14 @@
         att[pl.ds(0, half), at] = pltpu.roll(jnp.where(low, odd, even), HD, 1).astype(jnp.bfloat16)
         att[pl.ds(half, half), at] = jnp.where(low, even, odd).astype(jnp.bfloat16)
 
-    def project_out(j, c):
-        columns = pl.ds(pl.multiple_of(j * 256, 256), 256)
-        outv[:, columns] = dot(att[...], wo[:, columns]).astype(jnp.bfloat16)
-        return c
-
-    lax.fori_loop(0, width // 256, project_out, 0)
-    store = pltpu.make_async_copy(outv, out_hbm, out_sem)
+    store = pltpu.make_async_copy(att, out_hbm, out_sem)
     store.start()
 
     def wait_sends(i, c):
-        for name in ("c", "l", "q", "kv"):
+        for name in ("c", "l", "q"):
             view_copy(i, name).wait_send()
+        for part in range(CHUNKS):
+            view_copy(i, "kv", part).wait_send()
         o_copy(i).wait_send()
         return c
 
@@ -323,8 +332,9 @@
         return c
 
     def wait_forward_sends(i, c):
-        forward(i, 0).wait_send()
-        forward(i, 1).wait_send()
+        for part in range(CHUNKS):
+            forward(i, part, 0).wait_send()
+            forward(i, part, 1).wait_send()
         return c
 
     lax.fori_loop(1, nview, wait_sends, 0)
@@ -341,17 +351,16 @@
     most = epi_lists.shape[2]
     nblk = rows // BLK
     band = lax.axis_index("tok")
-    entry_view = epi_lists[0, :, :, 0].reshape(-1)
-    entry_block = epi_lists[0, :, :, 1].reshape(-1) - (band - 1) * nblk
+    entry_view = epi_lists[0, :, :, 0]
+    entry_block = epi_lists[0, :, :, 1] - (band - 1) * nblk
     place = ((entry_block // nblk) * nview + entry_view) * nblk + entry_block % nblk
     place = jnp.where(entry_view >= 0, place, 3 * nview * nblk)
-    lists = jnp.zeros((8, 128), jnp.int32).at[0, : nblk * most].set(place)
+    lists = jnp.pad(place, ((0, 8 - nblk), (0, 128 - most)))
     bf, f32 = jnp.bfloat16, jnp.float32
     half = rows // 2
     dma = pltpu.SemaphoreType.DMA
     scratch = [
         pltpu.VMEM((rows + crows, width), bf),
-        pltpu.VMEM((width, width), bf),
         pltpu.VMEM((width, width), bf),
         pltpu.VMEM((width, width), bf),
         pltpu.VMEM((width, width), bf),
@@ -371,25 +380,26 @@
         pltpu.VMEM((nview, half, 128), bf),
         pltpu.VMEM((nview, half, 128), bf),
         pltpu.VMEM((rows, width), bf),
-        pltpu.VMEM((rows, width), bf),
-        dma((7,)),
-        *[dma((nview,)) for _ in range(8)],
+        dma((6,)),
+        dma((nview,)), dma((nview,)),
+        dma((CHUNKS * nview,)), dma((CHUNKS * nview,)),
+        *[dma((nview,)) for _ in range(4)],
         dma((ntok,)), dma((ntok,)),
-        dma((2, nview)), dma((2, nview)),
+        dma((2, CHUNKS * nview)), dma((2, CHUNKS * nview)),
         dma((nview,)), dma((nview,)),
         dma, dma,
     ]
-    mixed = pl.pallas_call(
-        functools.partial(kernel, nview, ntok, rows, crows, most),
+    attended = pl.pallas_call(
+        functools.partial(kernel, nview, ntok, math.isqrt(nview), rows, crows, most),
         out_shape=jax.ShapeDtypeStruct((rows, width), bf),
-        in_specs=[pl.BlockSpec(memory_space=pl.ANY)] * 7,
+        in_specs=[pl.BlockSpec(memory_space=pl.ANY)] * 6,
         out_specs=pl.BlockSpec(memory_space=pl.ANY),
         scratch_shapes=scratch,
         compiler_params=pltpu.CompilerParams(
             collective_id=0, has_side_effects=True, vmem_limit_bytes=60 * 1024 * 1024
         ),
-    )(x_target[0], cond_x, w_query, w_key, w_value, w_out, lists)
-    return mixed[None]
+    )(x_target[0], cond_x, w_query, w_key, w_value, lists)
+    return dot(attended, w_out).astype(bf)[None]
 
 
 def solution(mesh):

time: 125 us -> 95.3 us (0.76); the launches traced: 123 us -> 95.2 us
  Pallas kernels: 119 us -> 90.2 us
  matrix products: 0 us -> 3.45 us
  local copies, waits for them, and re-layouts: 3.03 us -> 0.6 us
    pallas_call x1, Pallas kernels: 119 us -> 90.2 us  [local(): pl.pallas_call(functools.partial(kernel, nview, ntok, math.isqrt(nview),...]
    dot_general x0 -> x1, matrix products: none -> 3.45 us  [dot(): return jnp.dot(a, b, preferred_element_type=jnp.float32)]
    unnamed x1 -> x2, local copies, waits for them, and re-layouts: 2.26 us -> 0.01 us
where the time goes in v2:
time: 95.3 us; the launch traced here: 95.2 us
  Pallas kernels  90.2 us (95%)
  matrix products  3.45 us (4%)
    pallas_call x1, Pallas kernels, local(): pl.pallas_call(functools.partial(kernel, nview, ntok, math.isqrt(nview),...  90.2 us
    dot_general x1, matrix products, dot(): return jnp.dot(a, b, preferred_element_type=jnp.float32)  3.45 us

profile of v2, /device:TPU:33, one launch (start us, length us, event | category | flops | bytes accessed | tf_op | source)
XLA Modules:
  0.0 95.2 jit_solution(16397845029851305311)
XLA Ops:
  0.0 0.0 copy-start
  0.0 0.9 slice_subtract_fusion
  0.9 0.6 pad.4.lists_hbm
  1.5 90.2 %shard_map.73 = bf16[512,1024]{1,0:T(8,128)(2,1)} custom-call(bf16[512,1024]{1,0:T(8,128)(2,1)} %bitcast.7, bf16[16,1024]{1,0:T(8,128)(2,1)} %cond_hbm.1, bf16[1024,1024]{1,0:T(8,128)(2,1)} %wq_hbm.1, bf16[1024,1024]{1,0:T(8,128)(2,1)} %wk_hbm.1, bf16[1024,1024]{1,0:T(8,128)(2,1)} %wv_hbm.1, s32[8,128]{1,0:T(8,128)} %pad.4.lists_hbm), custom_call_target="tpu_custom_call" | custom-call | tf_op jit(solution)/shard_map/pallas_call | solution.py:392
  91.7 0.0 copy-done
  91.7 3.4 %fusion = bf16[1,512,1024]{2,1,0:T(8,128)(2,1)} fusion(bf16[512,1024]{1,0:T(8,128)(2,1)} %shard_map.73, bf16[1024,1024]{1,0:T(8,128)(2,1)S(1)} %copy-done), kind=kOutput, calls=%fused_computation.1 | convolution fusion | flops 1074266112 | bytes 4194304 | tf_op jit(solution)/shard_map/dot_general | solution.py:19
  (1 shorter events, 0.0 us)
Async XLA Ops:
  0.0 91.7 %copy-start = (bf16[1024,1024]{1,0:T(8,128)(2,1)S(1)}, bf16[1024,1024]{1,0:T(8,128)(2,1)}, u32[]{:S(2)}) copy-start(bf16[1024,1024]{1,0:T(8,128)(2,1)} %param.12) | copy-start | bytes 6291460

commit v3 on v2

v3 whole, which is shorter than its diff:
```python
import functools
import math

import jax
import jax.numpy as jnp
from jax import lax
from jax.experimental import pallas as pl
from jax.experimental.pallas import tpu as pltpu
from jax.sharding import PartitionSpec as P

HD = 64
BLK = 128
MESH = pl.DeviceIdType.MESH
LAG = 2
FIRST = 7
VPS = 2


def dot(a, b):
    return jnp.dot(a, b, preferred_element_type=jnp.float32)


def dot_t(a, b):
    return lax.dot_general(a, b, (((1,), (1,)), ((), ())), preferred_element_type=jnp.float32)


def kernel(
    nview, ntok, side, rows, crows, most,
    x_hbm, cond_hbm, wq_hbm, wk_hbm, wv_hbm, lists_hbm,
    out_hbm,
    xall, wq, wk, wv,
    qsend, ksend, vsend, csend, lsend,
    qrecv, kpool, vpool, condkv, lists_v, lists_s,
    vcond, qstk, acc_t, peak_t, osend, orecv, att,
    load_sem, q_ss, q_rs, kv_ss, kv_rs, c_ss, c_rs, l_ss, l_rs, g_ss, g_rs, f_ss, f_rs, o_ss, o_rs, smem_sem, out_sem,
):
    view = lax.axis_index("view")
    tok = lax.axis_index("tok")
    width = nview * HD
    half = rows // 2
    nblk = rows // BLK
    scale = math.log2(math.e) * HD ** -0.5

    loads = [
        pltpu.make_async_copy(x_hbm, xall.at[pl.ds(0, rows)], load_sem.at[0]),
        pltpu.make_async_copy(wq_hbm, wq, load_sem.at[1]),
        pltpu.make_async_copy(cond_hbm, xall.at[pl.ds(rows, crows)], load_sem.at[2]),
        pltpu.make_async_copy(wk_hbm, wk, load_sem.at[3]),
        pltpu.make_async_copy(wv_hbm, wv, load_sem.at[4]),
        pltpu.make_async_copy(lists_hbm, lsend, load_sem.at[5]),
    ]
    for load in loads:
        load.start()

    barrier = pltpu.get_barrier_semaphore()

    def peer(i, sign):
        dx, dy = lax.rem(i, side), lax.rem(i + i // side, side)
        x = lax.rem(view // side + sign * dx + side, side)
        y = lax.rem(lax.rem(view, side) + sign * dy + side, side)
        return x * side + y

    def greet_view(i, c):
        pl.semaphore_signal(barrier, inc=1, device_id=(peer(i, 1), tok), device_id_type=MESH)
        return c

    def greet_tok(i, c):
        pl.semaphore_signal(
            barrier, inc=1, device_id=(view, lax.rem(tok + i, ntok)), device_id_type=MESH
        )
        return c

    lax.fori_loop(1, nview, greet_view, 0)
    lax.fori_loop(1, ntok, greet_tok, 0)

    low = lax.broadcasted_iota(jnp.int32, (1, 2 * HD), 1) < HD

    def split(x, count):
        x = x.reshape(count, 2, -1, 2 * HD)
        first = x[:, 0].reshape(-1, 2 * HD)
        second = pltpu.roll(x[:, 1].reshape(-1, 2 * HD), HD, 1)
        even = jnp.where(low, first, second).astype(jnp.bfloat16)
        odd = jnp.where(low, second, first).astype(jnp.bfloat16)
        return even, odd

    def project_q(j, c):
        columns = pl.ds(pl.multiple_of(j * 256, 256), 256)
        query = dot(xall[pl.ds(0, rows), :], wq[:, columns])
        for p in range(2):
            even, odd = split(query[:, p * 128 : (p + 1) * 128], 1)
            qsend[4 * j + 2 * p] = even
            qsend[4 * j + 2 * p + 1] = odd
        return c

    loads[0].wait()
    loads[1].wait()
    lax.fori_loop(0, width // 256, project_q, 0)

    pl.semaphore_wait(barrier, nview + ntok - 2)

    def view_copy(i, name):
        to = peer(i, 1)
        target = (to, tok)

        def remote(src, dst, send, recv, at):
            return pltpu.make_async_remote_copy(
                src_ref=src, dst_ref=dst, send_sem=send.at[at], recv_sem=recv.at[at],
                device_id=target, device_id_type=MESH,
            )

        own = pl.ds((nview + view) * nblk, nblk)
        if name == "c":
            return remote(csend.at[to], condkv.at[tok, view], c_ss, c_rs, i)
        if name == "l":
            return remote(lsend, lists_v.at[view], l_ss, l_rs, i)
        if name == "q":
            return remote(qsend.at[to], qrecv.at[view], q_ss, q_rs, i)
        if name == "k":
            return remote(ksend.at[to], kpool.at[own], kv_ss, kv_rs, i)
        return remote(vsend.at[to], vpool.at[own], kv_ss, kv_rs, nview + i)

    def start(*names, lo=1, hi=nview):
        def body(i, c):
            for name in names:
                view_copy(i, name).start()
            return c

        lax.fori_loop(lo, hi, body, 0)

    start("q", hi=1 + FIRST)
    for load in loads[2:]:
        load.wait()

    def project_kv(j, c):
        columns = pl.ds(pl.multiple_of(j * 256, 256), 256)
        keys = dot(xall[...], wk[:, columns])
        values = dot(xall[...], wv[:, columns])
        for p in range(2):
            head = 4 * j + 2 * p
            k = keys[:, p * 128 : (p + 1) * 128]
            v = values[:, p * 128 : (p + 1) * 128]
            for send, x in ((ksend, k), (vsend, v)):
                even, odd = split(x[:rows], nblk)
                send[head] = even.reshape(nblk, BLK // 2, 2 * HD)
                send[head + 1] = odd.reshape(nblk, BLK // 2, 2 * HD)
            k, v = k[rows:], pltpu.roll(v[rows:], HD, 1)
            csend[head] = jnp.where(low, k, v).astype(jnp.bfloat16)
            csend[head + 1] = jnp.where(low, v, k).astype(jnp.bfloat16)
        return c

    lax.fori_loop(0, width // 256, project_kv, 0)
    start("c", "l")
    start("q", lo=1 + FIRST)
    start("k", "v")
    condkv[tok, view] = csend[view]
    lists_v[view] = lsend[...]
    qrecv[view] = qsend[view]
    kpool[pl.ds((nview + view) * nblk, nblk)] = ksend[view]
    vpool[pl.ds((nview + view) * nblk, nblk)] = vsend[view]

    def wait_view(name, start_i=1):
        def body(i, c):
            view_copy(i, name).wait_recv()
            return c

        lax.fori_loop(start_i, nview, body, 0)

    wait_view("c")

    def tok_copy(i):
        return pltpu.make_async_remote_copy(
            src_ref=condkv.at[tok], dst_ref=condkv.at[tok],
            send_sem=g_ss.at[i], recv_sem=g_rs.at[i],
            device_id=(view, lax.rem(tok + i, ntok)), device_id_type=MESH,
        )

    def start_tok(i, c):
        tok_copy(i).start()
        return c

    def wait_tok(i, c):
        tok_copy(i).wait_recv()
        return c

    lax.fori_loop(1, ntok, start_tok, 0)
    lax.fori_loop(1, ntok, wait_tok, 0)

    parity = lax.rem(view, 2)
    lane = lax.broadcasted_iota(jnp.int32, (1, 2 * HD), 1)
    khalf = (lane // HD) == parity
    kf = jnp.where(khalf, 1.0, 0.0)
    krow = kf.astype(jnp.bfloat16)
    vrow = (1.0 - kf).astype(jnp.bfloat16)
    count = ntok * nview * crows

    spare = condkv[0, pl.ds(0, BLK // crows)].reshape(BLK, 2 * HD).astype(jnp.float32)
    kpool[3 * nview * nblk] = jnp.where(
        khalf, spare[: BLK // 2], pltpu.roll(spare[BLK // 2 :], HD, 1)
    ).astype(jnp.bfloat16)
    vpool[3 * nview * nblk] = jnp.zeros((BLK // 2, 2 * HD), jnp.bfloat16)
    vcond[...] = condkv[...].reshape(count, 2 * HD) * vrow + krow

    def forward(i, part, direction):
        owner = peer(i, -1) * nblk
        pool = (kpool, vpool)[part]
        step = 1 if direction == 0 else ntok - 1
        sem = part * nview + i
        return pltpu.make_async_remote_copy(
            src_ref=pool.at[pl.ds(nview * nblk + owner, nblk)],
            dst_ref=pool.at[pl.ds(2 * direction * nview * nblk + owner, nblk)],
            send_sem=f_ss.at[direction, sem], recv_sem=f_rs.at[direction, sem],
            device_id=(view, lax.rem(tok + step, ntok)), device_id_type=MESH,
        )

    for part in range(2):
        forward(0, part, 0).start()
        forward(0, part, 1).start()

    def pass_on(i):
        for part, name in enumerate("kv"):
            view_copy(i, name).wait_recv()
            forward(i, part, 0).start()
            forward(i, part, 1).start()

    def cond_step(i, c):
        @pl.when(i > 0)
        def _():
            view_copy(i, "q").wait_recv()

        packed = qrecv[peer(i, -1)].astype(jnp.float32)
        rolled = pltpu.roll(packed, HD, 1)
        first = [
            jnp.where(khalf, packed, 0.0).astype(jnp.bfloat16),
            jnp.where(khalf, rolled, 0.0).astype(jnp.bfloat16),
        ]
        other = [
            jnp.where(khalf, 0.0, rolled).astype(jnp.bfloat16),
            jnp.where(khalf, 0.0, packed).astype(jnp.bfloat16),
        ]
        ck = condkv[...].reshape(count, 2 * HD)
        scores = [dot_t(first[part], ck) for part in range(2)]
        for part in range(2):
            peak = jnp.max(scores[part], axis=1, keepdims=True)
            weights = jnp.exp2((scores[part] - peak) * scale).astype(jnp.bfloat16)
            total = dot(weights, vcond[...])
            peak = jnp.broadcast_to(peak, (half, 2 * HD))
            for b in range(nblk // 2):
                at = slice(b * BLK, (b + 1) * BLK)
                to = part * (nblk // 2) + b
                qstk[i, to, pl.ds(0, BLK)] = first[part][at]
                qstk[i, to, pl.ds(BLK, BLK)] = other[part][at]
                turned = total[at].T
                acc_t[i, to, pl.ds(0, HD)] = jnp.where(parity == 0, turned[HD:], turned[:HD])
                acc_t[i, to, pl.ds(HD, 8)] = jnp.where(
                    parity == 0, turned[:8], turned[HD : HD + 8]
                )
                peak_t[i, to] = peak[at].T[:8]

        @pl.when(i > LAG)
        def _():
            pass_on(i - LAG)

        return c

    lax.fori_loop(0, nview, cond_step, 0)

    def rest(i, c):
        pass_on(i)
        return c

    lax.fori_loop(nview - LAG, nview, rest, 0)
    wait_view("l")
    to_smem = pltpu.make_async_copy(lists_v, lists_s, smem_sem)
    to_smem.start()
    to_smem.wait()

    def wait_forward(i, c):
        for part in range(2):
            forward(i, part, 0).wait_recv()
            forward(i, part, 1).wait_recv()
        return c

    lax.fori_loop(0, nview, wait_forward, 0)

    def o_copy(i):
        return pltpu.make_async_remote_copy(
            src_ref=osend.at[i], dst_ref=orecv.at[view],
            send_sem=o_ss.at[i], recv_sem=o_rs.at[i],
            device_id=(peer(i, -1), tok), device_id_type=MESH,
        )

    half_lane = lane < HD

    def epi_step(j, c):
        steps = [lax.rem(VPS * j + a + 1, nview) for a in range(VPS)]
        work = [(i, peer(i, -1), b) for i in steps for b in range(nblk)]
        unused = 3 * nview * nblk
        scores, parts = [], []
        for i, owner, b in work:
            keys = jnp.concatenate([kpool[lists_s[owner, b, s]] for s in range(most)], axis=0)
            scores.append(dot_t(keys, qstk[i, b]))
        for (i, owner, b), score in zip(work, scores):
            before = peak_t[i, b][:1]
            peak = jnp.max(score, axis=0, keepdims=True)
            peak = jnp.maximum(jnp.maximum(peak[:, :BLK], peak[:, BLK:]), before)
            weights = jnp.exp2((score - jnp.concatenate([peak, peak], axis=1)) * scale)
            weights = weights.astype(jnp.bfloat16)
            fade = jnp.exp2((before - peak) * scale)
            entries = [lists_s[owner, b, s] for s in range(most)]
            used = [jnp.where(entry < unused, 1.0, 0.0) for entry in entries]
            values = jnp.concatenate([vpool[entry] for entry in entries], axis=0)
            sums = jnp.concatenate(
                [
                    jnp.broadcast_to(jnp.where(half_lane, used[s], used[s + 1]), (16, 2 * HD))
                    for s in range(0, most, 2)
                ],
                axis=1,
            ).astype(jnp.bfloat16)
            top = lax.dot_general(
                values, weights, (((0,), (0,)), ((), ())), preferred_element_type=jnp.float32
            )
            ones = dot(sums, weights)
            part = jnp.where(
                parity == 0,
                top[:HD, :BLK] + top[HD:, BLK:],
                top[HD:, :BLK] + top[:HD, BLK:],
            )
            total = ones[:1, :BLK] + ones[:1, BLK:] + acc_t[i, b, pl.ds(HD, 8)][:1] * fade
            parts.append((part + acc_t[i, b, pl.ds(0, HD)] * fade) / total)
        for a, i in enumerate(steps):
            mine = parts[a * nblk : (a + 1) * nblk]
            for b in range(nblk // 2):
                pair = jnp.concatenate([mine[b], mine[b + nblk // 2]], axis=0)
                osend[i, pl.ds(b * BLK, BLK)] = pair.T.astype(jnp.bfloat16)
            if a < VPS - 1:
                o_copy(i).start()
            else:

                @pl.when(i > 0)
                def _():
                    o_copy(i).start()

                @pl.when(i == 0)
                def _():
                    orecv[view] = osend[i]

        return c

    lax.fori_loop(0, nview // VPS, epi_step, 0)

    def wait_o(i, c):
        o_copy(i).wait_recv()
        return c

    lax.fori_loop(1, nview, wait_o, 0)

    for j in range(nview // 2):
        even = orecv[2 * j].astype(jnp.float32)
        odd = orecv[2 * j + 1].astype(jnp.float32)
        at = pl.ds(j * 128, 128)
        att[pl.ds(0, half), at] = jnp.where(low, even, pltpu.roll(odd, HD, 1)).astype(jnp.bfloat16)
        att[pl.ds(half, half), at] = jnp.where(low, pltpu.roll(even, HD, 1), odd).astype(
            jnp.bfloat16
        )

    store = pltpu.make_async_copy(att, out_hbm, out_sem)
    store.start()

    def wait_sends(i, c):
        for name in ("c", "l", "q", "k", "v"):
            view_copy(i, name).wait_send()
        o_copy(i).wait_send()
        return c

    def wait_tok_sends(i, c):
        tok_copy(i).wait_send()
        return c

    def wait_forward_sends(i, c):
        for part in range(2):
            forward(i, part, 0).wait_send()
            forward(i, part, 1).wait_send()
        return c

    lax.fori_loop(1, nview, wait_sends, 0)
    lax.fori_loop(1, ntok, wait_tok_sends, 0)
    lax.fori_loop(0, nview, wait_forward_sends, 0)
    store.wait()


def local(x_target, cond_x, w_query, w_key, w_value, w_out, epi_lists):
    nview = lax.axis_size("view")
    ntok = lax.axis_size("tok")
    rows, width = x_target.shape[1:]
    crows = cond_x.shape[0]
    most = epi_lists.shape[2]
    nblk = rows // BLK
    band = lax.axis_index("tok")
    entry_view = epi_lists[0, :, :, 0]
    entry_block = epi_lists[0, :, :, 1] - (band - 1) * nblk
    place = ((entry_block // nblk) * nview + entry_view) * nblk + entry_block % nblk
    place = jnp.where(entry_view >= 0, place, 3 * nview * nblk)
    lists = jnp.pad(place, ((0, 8 - nblk), (0, 128 - most)))
    bf, f32 = jnp.bfloat16, jnp.float32
    half = rows // 2
    dma = pltpu.SemaphoreType.DMA
    scratch = [
        pltpu.VMEM((rows + crows, width), bf),
        pltpu.VMEM((width, width), bf),
        pltpu.VMEM((width, width), bf),
        pltpu.VMEM((width, width), bf),
        pltpu.VMEM((nview, half, 128), bf),
        pltpu.VMEM((nview, nblk, BLK // 2, 128), bf),
        pltpu.VMEM((nview, nblk, BLK // 2, 128), bf),
        pltpu.VMEM((nview, crows, 128), bf),
        pltpu.VMEM((8, 128), jnp.int32),
        pltpu.VMEM((nview, half, 128), bf),
        pltpu.VMEM((3 * nview * nblk + 1, BLK // 2, 128), bf),
        pltpu.VMEM((3 * nview * nblk + 1, BLK // 2, 128), bf),
        pltpu.VMEM((ntok, nview, crows, 128), bf),
        pltpu.VMEM((nview, 8, 128), jnp.int32),
        pltpu.SMEM((nview, 8, 128), jnp.int32),
        pltpu.VMEM((ntok * nview * crows, 128), bf),
        pltpu.VMEM((nview, nblk, 2 * BLK, 128), bf),
        pltpu.VMEM((nview, nblk, HD + 8, BLK), f32),
        pltpu.VMEM((nview, nblk, 8, BLK), f32),
        pltpu.VMEM((nview, half, 128), bf),
        pltpu.VMEM((nview, half, 128), bf),
        pltpu.VMEM((rows, width), bf),
        dma((6,)),
        dma((nview,)), dma((nview,)),
        dma((2 * nview,)), dma((2 * nview,)),
        *[dma((nview,)) for _ in range(4)],
        dma((ntok,)), dma((ntok,)),
        dma((2, 2 * nview)), dma((2, 2 * nview)),
        dma((nview,)), dma((nview,)),
        dma, dma,
    ]
    attended = pl.pallas_call(
        functools.partial(kernel, nview, ntok, math.isqrt(nview), rows, crows, most),
        out_shape=jax.ShapeDtypeStruct((rows, width), bf),
        in_specs=[pl.BlockSpec(memory_space=pl.ANY)] * 6,
        out_specs=pl.BlockSpec(memory_space=pl.ANY),
        scratch_shapes=scratch,
        compiler_params=pltpu.CompilerParams(
            collective_id=0, has_side_effects=True, vmem_limit_bytes=60 * 1024 * 1024
        ),
    )(x_target[0], cond_x, w_query, w_key, w_value, lists)
    return dot(attended, w_out).astype(bf)[None]


def solution(mesh):
    placed = (
        P("view", "tok", None),
        P(("view", "tok"), None),
        P(),
        P(),
        P(),
        P(),
        P("view", "tok", None, None),
    )
    return jax.shard_map(
        local, mesh=mesh, in_specs=placed, out_specs=P("view", "tok", None), check_vma=False
    )
```

time: 95.3 us -> 86.9 us (0.912); the launches traced: 95.2 us -> 85.7 us
  Pallas kernels: 90.2 us -> 80.8 us
    pallas_call x1, Pallas kernels: 90.2 us -> 80.8 us  [local(): pl.pallas_call(functools.partial(kernel, nview, ntok, math.isqrt(nview),...]
where the time goes in v3:
time: 86.9 us; the launch traced here: 85.7 us
  Pallas kernels  80.8 us (93%)
  matrix products  3.45 us (4%)
  other arithmetic  0.88 us (1%)
    pallas_call x1, Pallas kernels, local(): pl.pallas_call(functools.partial(kernel, nview, ntok, math.isqrt(nview),...  80.8 us
    dot_general x1, matrix products, dot(): return jnp.dot(a, b, preferred_element_type=jnp.float32)  3.45 us

profile of v3, /device:TPU:33, one launch (start us, length us, event | category | flops | bytes accessed | tf_op | source)
XLA Modules:
  0.0 85.7 jit_solution(6684801656686616258)
XLA Ops:
  0.0 0.0 copy-start
  0.0 0.9 %slice_subtract_fusion = (s32[1,4,8,1]{2,3,1,0:T(1,128)S(1)}, s32[1,4,8,1]{2,3,1,0:T(1,128)S(1)}) fusion(s32[1,4,8,2]{2,3,1,0:T(2,128)} %param.13, s32[]{:T(128)S(6)} %mul.13), kind=kLoop, calls=%fused_computation.13 | loop fusion | flops 32 | bytes 516 | tf_op jit(solution)/shard_map/sub | solution.py:400
  0.9 0.6 pad.4.lists_hbm
  1.5 80.8 %shard_map.73 = bf16[512,1024]{1,0:T(8,128)(2,1)} custom-call(bf16[512,1024]{1,0:T(8,128)(2,1)} %bitcast.7, bf16[16,1024]{1,0:T(8,128)(2,1)} %cond_hbm.1, bf16[1024,1024]{1,0:T(8,128)(2,1)} %wq_hbm.1, bf16[1024,1024]{1,0:T(8,128)(2,1)} %wk_hbm.1, bf16[1024,1024]{1,0:T(8,128)(2,1)} %wv_hbm.1, s32[8,128]{1,0:T(8,128)} %pad.4.lists_hbm), custom_call_target="tpu_custom_call" | custom-call | tf_op jit(solution)/shard_map/pallas_call | solution.py:439
  82.3 0.0 copy-done
  82.3 3.4 %fusion = bf16[1,512,1024]{2,1,0:T(8,128)(2,1)} fusion(bf16[512,1024]{1,0:T(8,128)(2,1)} %shard_map.73, bf16[1024,1024]{1,0:T(8,128)(2,1)S(1)} %copy-done), kind=kOutput, calls=%fused_computation.1 | convolution fusion | flops 1074266112 | bytes 4194304 | tf_op jit(solution)/shard_map/dot_general | solution.py:20
  (1 shorter events, 0.0 us)
Async XLA Ops:
  0.0 82.3 %copy-start = (bf16[1024,1024]{1,0:T(8,128)(2,1)S(1)}, bf16[1024,1024]{1,0:T(8,128)(2,1)}, u32[]{:S(2)}) copy-start(bf16[1024,1024]{1,0:T(8,128)(2,1)} %param.12) | copy-start | bytes 6291460

commit v4 on v3

--- a/solution.py
+++ b/solution.py
@@ -29,7 +29,7 @@
     x_hbm, cond_hbm, wq_hbm, wk_hbm, wv_hbm, lists_hbm,
     out_hbm,
     xall, wq, wk, wv,
-    qsend, ksend, vsend, csend, lsend,
+    qsend, ksend, vsend, csend, lraw, lsend,
     qrecv, kpool, vpool, condkv, lists_v, lists_s,
     vcond, qstk, acc_t, peak_t, osend, orecv, att,
     load_sem, q_ss, q_rs, kv_ss, kv_rs, c_ss, c_rs, l_ss, l_rs, g_ss, g_rs, f_ss, f_rs, o_ss, o_rs, smem_sem, out_sem,
@@ -47,7 +47,7 @@
         pltpu.make_async_copy(cond_hbm, xall.at[pl.ds(rows, crows)], load_sem.at[2]),
         pltpu.make_async_copy(wk_hbm, wk, load_sem.at[3]),
         pltpu.make_async_copy(wv_hbm, wv, load_sem.at[4]),
-        pltpu.make_async_copy(lists_hbm, lsend, load_sem.at[5]),
+        pltpu.make_async_copy(lists_hbm, lraw, load_sem.at[5]),
     ]
     for load in loads:
         load.start()
@@ -149,6 +149,14 @@
         return c
 
     lax.fori_loop(0, width // 256, project_kv, 0)
+    raw = lraw[...]
+    entry_view, entry_block = raw[:, 0, :], raw[:, 1, :] - (tok - 1) * nblk
+    band, inner = entry_block // nblk, lax.rem(entry_block, nblk)
+    place = (band * nview + entry_view) * nblk + inner
+    place = jnp.where(entry_view >= 0, place, 3 * nview * nblk)
+    place = jnp.clip(place, 0, 3 * nview * nblk)
+    lsend[...] = jnp.zeros((8, 128), jnp.int32)
+    lsend[pl.ds(0, nblk), pl.ds(0, most)] = place
     start("c", "l")
     start("q", lo=1 + FIRST)
     start("k", "v")
@@ -395,12 +403,7 @@
     crows = cond_x.shape[0]
     most = epi_lists.shape[2]
     nblk = rows // BLK
-    band = lax.axis_index("tok")
-    entry_view = epi_lists[0, :, :, 0]
-    entry_block = epi_lists[0, :, :, 1] - (band - 1) * nblk
-    place = ((entry_block // nblk) * nview + entry_view) * nblk + entry_block % nblk
-    place = jnp.where(entry_view >= 0, place, 3 * nview * nblk)
-    lists = jnp.pad(place, ((0, 8 - nblk), (0, 128 - most)))
+    lists = jnp.transpose(epi_lists[0], (0, 2, 1))
     bf, f32 = jnp.bfloat16, jnp.float32
     half = rows // 2
     dma = pltpu.SemaphoreType.DMA
@@ -413,6 +416,7 @@
         pltpu.VMEM((nview, nblk, BLK // 2, 128), bf),
         pltpu.VMEM((nview, nblk, BLK // 2, 128), bf),
         pltpu.VMEM((nview, crows, 128), bf),
+        pltpu.VMEM((nblk, 2, most), jnp.int32),
         pltpu.VMEM((8, 128), jnp.int32),
         pltpu.VMEM((nview, half, 128), bf),
         pltpu.VMEM((3 * nview * nblk + 1, BLK // 2, 128), bf),

time: 86.9 us -> 85.7 us (0.986)
  other arithmetic: 0.88 us -> 0 us
where the time goes in v4:
time: 85.7 us; the launch traced here: 84.3 us
  Pallas kernels  80.9 us (94%)
  matrix products  3.45 us (4%)
    pallas_call x1, Pallas kernels, local(): pl.pallas_call(functools.partial(kernel, nview, ntok, math.isqrt(nview),...  80.9 us
    dot_general x1, matrix products, dot(): return jnp.dot(a, b, preferred_element_type=jnp.float32)  3.45 us

profile of v4, /device:TPU:33, one launch (start us, length us, event | category | flops | bytes accessed | tf_op | source)
XLA Modules:
  0.0 84.3 jit_solution(53960031937461451)
XLA Ops:
  0.0 0.0 copy-start
  0.0 80.9 %shard_map.73 = bf16[512,1024]{1,0:T(8,128)(2,1)} custom-call(bf16[512,1024]{1,0:T(8,128)(2,1)} %bitcast.8, bf16[16,1024]{1,0:T(8,128)(2,1)} %cond_hbm.1, bf16[1024,1024]{1,0:T(8,128)(2,1)} %wq_hbm.1, bf16[1024,1024]{1,0:T(8,128)(2,1)} %wk_hbm.1, bf16[1024,1024]{1,0:T(8,128)(2,1)} %wv_hbm.1, s32[4,2,8]{2,1,0:T(2,128)} %bitcast.9), custom_call_target="tpu_custom_call" | custom-call | tf_op jit(solution)/shard_map/pallas_call | solution.py:443
  80.9 0.0 copy-done
  80.9 3.4 %fusion = bf16[1,512,1024]{2,1,0:T(8,128)(2,1)} fusion(bf16[512,1024]{1,0:T(8,128)(2,1)} %shard_map.73, bf16[1024,1024]{1,0:T(8,128)(2,1)S(1)} %copy-done), kind=kOutput, calls=%fused_computation.1 | convolution fusion | flops 1074266112 | bytes 4194304 | tf_op jit(solution)/shard_map/dot_general | solution.py:20
Async XLA Ops:
  0.0 80.9 %copy-start = (bf16[1024,1024]{1,0:T(8,128)(2,1)S(1)}, bf16[1024,1024]{1,0:T(8,128)(2,1)}, u32[]{:S(2)}) copy-start(bf16[1024,1024]{1,0:T(8,128)(2,1)} %param.12) | copy-start | bytes 6291460

commit v5 on v4

--- a/solution.py
+++ b/solution.py
@@ -324,10 +324,8 @@
                 ],
                 axis=1,
             ).astype(jnp.bfloat16)
-            top = lax.dot_general(
-                values, weights, (((0,), (0,)), ((), ())), preferred_element_type=jnp.float32
-            )
-            ones = dot(sums, weights)
+            both = dot(jnp.concatenate([values.T, sums], axis=0), weights)
+            top, ones = both[: 2 * HD], both[2 * HD :]
             part = jnp.where(
                 parity == 0,
                 top[:HD, :BLK] + top[HD:, BLK:],

time: 85.7 us -> 84.4 us (0.985)
  Pallas kernels: 80.9 us -> 79.5 us
    pallas_call x1, Pallas kernels: 80.9 us -> 79.5 us  [local(): pl.pallas_call(functools.partial(kernel, nview, ntok, math.isqrt(nview),...]
where the time goes in v5:
time: 84.4 us; the launch traced here: 83 us
  Pallas kernels  79.5 us (94%)
  matrix products  3.45 us (4%)
    pallas_call x1, Pallas kernels, local(): pl.pallas_call(functools.partial(kernel, nview, ntok, math.isqrt(nview),...  79.5 us
    dot_general x1, matrix products, dot(): return jnp.dot(a, b, preferred_element_type=jnp.float32)  3.45 us

profile of v5, /device:TPU:33, one launch (start us, length us, event | category | flops | bytes accessed | tf_op | source)
XLA Modules:
  0.0 83.0 jit_solution(3088403003192866222)
XLA Ops:
  0.0 0.0 copy-start
  0.0 79.5 %shard_map.73 = bf16[512,1024]{1,0:T(8,128)(2,1)} custom-call(bf16[512,1024]{1,0:T(8,128)(2,1)} %bitcast.8, bf16[16,1024]{1,0:T(8,128)(2,1)} %cond_hbm.1, bf16[1024,1024]{1,0:T(8,128)(2,1)} %wq_hbm.1, bf16[1024,1024]{1,0:T(8,128)(2,1)} %wk_hbm.1, bf16[1024,1024]{1,0:T(8,128)(2,1)} %wv_hbm.1, s32[4,2,8]{2,1,0:T(2,128)} %bitcast.9), custom_call_target="tpu_custom_call" | custom-call | tf_op jit(solution)/shard_map/pallas_call | solution.py:441
  79.5 0.0 copy-done
  79.5 3.4 %fusion = bf16[1,512,1024]{2,1,0:T(8,128)(2,1)} fusion(bf16[512,1024]{1,0:T(8,128)(2,1)} %shard_map.73, bf16[1024,1024]{1,0:T(8,128)(2,1)S(1)} %copy-done), kind=kOutput, calls=%fused_computation.1 | convolution fusion | flops 1074266112 | bytes 4194304 | tf_op jit(solution)/shard_map/dot_general | solution.py:20
Async XLA Ops:
  0.0 79.5 %copy-start = (bf16[1024,1024]{1,0:T(8,128)(2,1)S(1)}, bf16[1024,1024]{1,0:T(8,128)(2,1)}, u32[]{:S(2)}) copy-start(bf16[1024,1024]{1,0:T(8,128)(2,1)} %param.12) | copy-start | bytes 6291460

commit v6 on v5

--- a/solution.py
+++ b/solution.py
@@ -11,7 +11,7 @@
 HD = 64
 BLK = 128
 MESH = pl.DeviceIdType.MESH
-LAG = 2
+LAG = 1
 FIRST = 7
 VPS = 2
 
@@ -29,8 +29,8 @@
     x_hbm, cond_hbm, wq_hbm, wk_hbm, wv_hbm, lists_hbm,
     out_hbm,
     xall, wq, wk, wv,
-    qsend, ksend, vsend, csend, lraw, lsend,
-    qrecv, kpool, vpool, condkv, lists_v, lists_s,
+    qsend, kvsend, csend, lraw, lsend,
+    qrecv, pool, condkv, lists_v, lists_s,
     vcond, qstk, acc_t, peak_t, osend, orecv, att,
     load_sem, q_ss, q_rs, kv_ss, kv_rs, c_ss, c_rs, l_ss, l_rs, g_ss, g_rs, f_ss, f_rs, o_ss, o_rs, smem_sem, out_sem,
 ):
@@ -40,6 +40,7 @@
     half = rows // 2
     nblk = rows // BLK
     scale = math.log2(math.e) * HD ** -0.5
+    unused = 3 * nview * 2 * nblk
 
     loads = [
         pltpu.make_async_copy(x_hbm, xall.at[pl.ds(0, rows)], load_sem.at[0]),
@@ -108,16 +109,14 @@
                 device_id=target, device_id_type=MESH,
             )
 
-        own = pl.ds((nview + view) * nblk, nblk)
+        own = pl.ds((nview + view) * 2 * nblk, 2 * nblk)
         if name == "c":
             return remote(csend.at[to], condkv.at[tok, view], c_ss, c_rs, i)
         if name == "l":
             return remote(lsend, lists_v.at[view], l_ss, l_rs, i)
         if name == "q":
             return remote(qsend.at[to], qrecv.at[view], q_ss, q_rs, i)
-        if name == "k":
-            return remote(ksend.at[to], kpool.at[own], kv_ss, kv_rs, i)
-        return remote(vsend.at[to], vpool.at[own], kv_ss, kv_rs, nview + i)
+        return remote(kvsend.at[to], pool.at[own], kv_ss, kv_rs, i)
 
     def start(*names, lo=1, hi=nview):
         def body(i, c):
@@ -139,10 +138,10 @@
             head = 4 * j + 2 * p
             k = keys[:, p * 128 : (p + 1) * 128]
             v = values[:, p * 128 : (p + 1) * 128]
-            for send, x in ((ksend, k), (vsend, v)):
+            for at, x in ((pl.ds(0, nblk), k), (pl.ds(nblk, nblk), v)):
                 even, odd = split(x[:rows], nblk)
-                send[head] = even.reshape(nblk, BLK // 2, 2 * HD)
-                send[head + 1] = odd.reshape(nblk, BLK // 2, 2 * HD)
+                kvsend[head, at] = even.reshape(nblk, BLK // 2, 2 * HD)
+                kvsend[head + 1, at] = odd.reshape(nblk, BLK // 2, 2 * HD)
             k, v = k[rows:], pltpu.roll(v[rows:], HD, 1)
             csend[head] = jnp.where(low, k, v).astype(jnp.bfloat16)
             csend[head + 1] = jnp.where(low, v, k).astype(jnp.bfloat16)
@@ -152,19 +151,18 @@
     raw = lraw[...]
     entry_view, entry_block = raw[:, 0, :], raw[:, 1, :] - (tok - 1) * nblk
     band, inner = entry_block // nblk, lax.rem(entry_block, nblk)
-    place = (band * nview + entry_view) * nblk + inner
-    place = jnp.where(entry_view >= 0, place, 3 * nview * nblk)
-    place = jnp.clip(place, 0, 3 * nview * nblk)
+    place = (band * nview + entry_view) * 2 * nblk + inner
+    place = jnp.where(entry_view >= 0, place, unused)
+    place = jnp.clip(place, 0, unused)
     lsend[...] = jnp.zeros((8, 128), jnp.int32)
     lsend[pl.ds(0, nblk), pl.ds(0, most)] = place
     start("c", "l")
     start("q", lo=1 + FIRST)
-    start("k", "v")
+    start("kv")
     condkv[tok, view] = csend[view]
     lists_v[view] = lsend[...]
     qrecv[view] = qsend[view]
-    kpool[pl.ds((nview + view) * nblk, nblk)] = ksend[view]
-    vpool[pl.ds((nview + view) * nblk, nblk)] = vsend[view]
+    pool[pl.ds((nview + view) * 2 * nblk, 2 * nblk)] = kvsend[view]
 
     def wait_view(name, start_i=1):
         def body(i, c):
@@ -202,33 +200,29 @@
     count = ntok * nview * crows
 
     spare = condkv[0, pl.ds(0, BLK // crows)].reshape(BLK, 2 * HD).astype(jnp.float32)
-    kpool[3 * nview * nblk] = jnp.where(
+    pool[unused] = jnp.where(
         khalf, spare[: BLK // 2], pltpu.roll(spare[BLK // 2 :], HD, 1)
     ).astype(jnp.bfloat16)
-    vpool[3 * nview * nblk] = jnp.zeros((BLK // 2, 2 * HD), jnp.bfloat16)
+    pool[unused + nblk] = jnp.zeros((BLK // 2, 2 * HD), jnp.bfloat16)
     vcond[...] = condkv[...].reshape(count, 2 * HD) * vrow + krow
 
-    def forward(i, part, direction):
-        owner = peer(i, -1) * nblk
-        pool = (kpool, vpool)[part]
+    def forward(i, direction):
+        owner = peer(i, -1) * 2 * nblk
         step = 1 if direction == 0 else ntok - 1
-        sem = part * nview + i
         return pltpu.make_async_remote_copy(
-            src_ref=pool.at[pl.ds(nview * nblk + owner, nblk)],
-            dst_ref=pool.at[pl.ds(2 * direction * nview * nblk + owner, nblk)],
-            send_sem=f_ss.at[direction, sem], recv_sem=f_rs.at[direction, sem],
+            src_ref=pool.at[pl.ds(nview * 2 * nblk + owner, 2 * nblk)],
+            dst_ref=pool.at[pl.ds(2 * direction * nview * 2 * nblk + owner, 2 * nblk)],
+            send_sem=f_ss.at[direction, i], recv_sem=f_rs.at[direction, i],
             device_id=(view, lax.rem(tok + step, ntok)), device_id_type=MESH,
         )
 
-    for part in range(2):
-        forward(0, part, 0).start()
-        forward(0, part, 1).start()
+    forward(0, 0).start()
+    forward(0, 1).start()
 
     def pass_on(i):
-        for part, name in enumerate("kv"):
-            view_copy(i, name).wait_recv()
-            forward(i, part, 0).start()
-            forward(i, part, 1).start()
+        view_copy(i, "kv").wait_recv()
+        forward(i, 0).start()
+        forward(i, 1).start()
 
     def cond_step(i, c):
         @pl.when(i > 0)
@@ -283,9 +277,8 @@
     to_smem.wait()
 
     def wait_forward(i, c):
-        for part in range(2):
-            forward(i, part, 0).wait_recv()
-            forward(i, part, 1).wait_recv()
+        forward(i, 0).wait_recv()
+        forward(i, 1).wait_recv()
         return c
 
     lax.fori_loop(0, nview, wait_forward, 0)
@@ -302,10 +295,9 @@
     def epi_step(j, c):
         steps = [lax.rem(VPS * j + a + 1, nview) for a in range(VPS)]
         work = [(i, peer(i, -1), b) for i in steps for b in range(nblk)]
-        unused = 3 * nview * nblk
         scores, parts = [], []
         for i, owner, b in work:
-            keys = jnp.concatenate([kpool[lists_s[owner, b, s]] for s in range(most)], axis=0)
+            keys = jnp.concatenate([pool[lists_s[owner, b, s]] for s in range(most)], axis=0)
             scores.append(dot_t(keys, qstk[i, b]))
         for (i, owner, b), score in zip(work, scores):
             before = peak_t[i, b][:1]
@@ -316,7 +308,7 @@
             fade = jnp.exp2((before - peak) * scale)
             entries = [lists_s[owner, b, s] for s in range(most)]
             used = [jnp.where(entry < unused, 1.0, 0.0) for entry in entries]
-            values = jnp.concatenate([vpool[entry] for entry in entries], axis=0)
+            values = jnp.concatenate([pool[entry + nblk] for entry in entries], axis=0)
             sums = jnp.concatenate(
                 [
                     jnp.broadcast_to(jnp.where(half_lane, used[s], used[s + 1]), (16, 2 * HD))
@@ -373,7 +365,7 @@
     store.start()
 
     def wait_sends(i, c):
-        for name in ("c", "l", "q", "k", "v"):
+        for name in ("c", "l", "q", "kv"):
             view_copy(i, name).wait_send()
         o_copy(i).wait_send()
         return c
@@ -383,9 +375,8 @@
         return c
 
     def wait_forward_sends(i, c):
-        for part in range(2):
-            forward(i, part, 0).wait_send()
-            forward(i, part, 1).wait_send()
+        forward(i, 0).wait_send()
+        forward(i, 1).wait_send()
         return c
 
     lax.fori_loop(1, nview, wait_sends, 0)
@@ -411,14 +402,12 @@
         pltpu.VMEM((width, width), bf),
         pltpu.VMEM((width, width), bf),
         pltpu.VMEM((nview, half, 128), bf),
-        pltpu.VMEM((nview, nblk, BLK // 2, 128), bf),
-        pltpu.VMEM((nview, nblk, BLK // 2, 128), bf),
+        pltpu.VMEM((nview, 2 * nblk, BLK // 2, 128), bf),
         pltpu.VMEM((nview, crows, 128), bf),
         pltpu.VMEM((nblk, 2, most), jnp.int32),
         pltpu.VMEM((8, 128), jnp.int32),
         pltpu.VMEM((nview, half, 128), bf),
-        pltpu.VMEM((3 * nview * nblk + 1, BLK // 2, 128), bf),
-        pltpu.VMEM((3 * nview * nblk + 1, BLK // 2, 128), bf),
+        pltpu.VMEM((3 * nview * 2 * nblk + nblk + 1, BLK // 2, 128), bf),
         pltpu.VMEM((ntok, nview, crows, 128), bf),
         pltpu.VMEM((nview, 8, 128), jnp.int32),
         pltpu.SMEM((nview, 8, 128), jnp.int32),
@@ -431,10 +420,10 @@
         pltpu.VMEM((rows, width), bf),
         dma((6,)),
         dma((nview,)), dma((nview,)),
-        dma((2 * nview,)), dma((2 * nview,)),
+        dma((nview,)), dma((nview,)),
         *[dma((nview,)) for _ in range(4)],
         dma((ntok,)), dma((ntok,)),
-        dma((2, 2 * nview)), dma((2, 2 * nview)),
+        dma((2, nview)), dma((2, nview)),
         dma((nview,)), dma((nview,)),
         dma, dma,
     ]

time: 84.4 us -> 83.4 us (0.988)
  the two profiles are of different devices: /device:TPU:33 before, /device:TPU:0 now
where the time goes in v6:
time: 83.4 us; the launch traced here: 83.3 us
  Pallas kernels  79.8 us (96%)
  matrix products  3.45 us (4%)
    pallas_call x1, Pallas kernels, local(): pl.pallas_call(functools.partial(kernel, nview, ntok, math.isqrt(nview),...  79.8 us
    dot_general x1, matrix products, dot(): return jnp.dot(a, b, preferred_element_type=jnp.float32)  3.45 us

profile of v6, /device:TPU:0, one launch (start us, length us, event | category | flops | bytes accessed | tf_op | source)
XLA Modules:
  0.0 83.3 jit_solution(13590352518717001064)
XLA Ops:
  0.0 0.0 copy-start
  0.0 79.8 %shard_map.73 = bf16[512,1024]{1,0:T(8,128)(2,1)} custom-call(bf16[512,1024]{1,0:T(8,128)(2,1)} %bitcast.8, bf16[16,1024]{1,0:T(8,128)(2,1)} %cond_hbm.1, bf16[1024,1024]{1,0:T(8,128)(2,1)} %wq_hbm.1, bf16[1024,1024]{1,0:T(8,128)(2,1)} %wk_hbm.1, bf16[1024,1024]{1,0:T(8,128)(2,1)} %wv_hbm.1, s32[4,2,8]{2,1,0:T(2,128)} %bitcast.9), custom_call_target="tpu_custom_call" | custom-call | tf_op jit(solution)/shard_map/pallas_call | solution.py:430
  79.8 0.0 copy-done
  79.8 3.4 %fusion = bf16[1,512,1024]{2,1,0:T(8,128)(2,1)} fusion(bf16[512,1024]{1,0:T(8,128)(2,1)} %shard_map.73, bf16[1024,1024]{1,0:T(8,128)(2,1)S(1)} %copy-done), kind=kOutput, calls=%fused_computation.1 | convolution fusion | flops 1074266112 | bytes 4194304 | tf_op jit(solution)/shard_map/dot_general | solution.py:20
Async XLA Ops:
  0.0 79.8 %copy-start = (bf16[1024,1024]{1,0:T(8,128)(2,1)S(1)}, bf16[1024,1024]{1,0:T(8,128)(2,1)}, u32[]{:S(2)}) copy-start(bf16[1024,1024]{1,0:T(8,128)(2,1)} %param.12) | copy-start | bytes 6291460

commit v7 on v6

--- a/solution.py
+++ b/solution.py
@@ -13,7 +13,7 @@
 MESH = pl.DeviceIdType.MESH
 LAG = 1
 FIRST = 7
-VPS = 2
+VPS = 4
 
 
 def dot(a, b):

time: 83.4 us -> 82.9 us (level)
  the two profiles are of different devices: /device:TPU:0 before, /device:TPU:33 now
where the time goes in v7:
time: 82.9 us; the launch traced here: 81.3 us
  Pallas kernels  77.8 us (94%)
  matrix products  3.45 us (4%)
    pallas_call x1, Pallas kernels, local(): pl.pallas_call(functools.partial(kernel, nview, ntok, math.isqrt(nview),...  77.8 us
    dot_general x1, matrix products, dot(): return jnp.dot(a, b, preferred_element_type=jnp.float32)  3.45 us

profile of v7, /device:TPU:33, one launch (start us, length us, event | category | flops | bytes accessed | tf_op | source)
XLA Modules:
  0.0 81.3 jit_solution(11171137423407234413)
XLA Ops:
  0.0 0.0 copy-start
  0.0 77.8 %shard_map.73 = bf16[512,1024]{1,0:T(8,128)(2,1)} custom-call(bf16[512,1024]{1,0:T(8,128)(2,1)} %bitcast.8, bf16[16,1024]{1,0:T(8,128)(2,1)} %cond_hbm.1, bf16[1024,1024]{1,0:T(8,128)(2,1)} %wq_hbm.1, bf16[1024,1024]{1,0:T(8,128)(2,1)} %wk_hbm.1, bf16[1024,1024]{1,0:T(8,128)(2,1)} %wv_hbm.1, s32[4,2,8]{2,1,0:T(2,128)} %bitcast.9), custom_call_target="tpu_custom_call" | custom-call | tf_op jit(solution)/shard_map/pallas_call | solution.py:430
  77.8 0.0 copy-done
  77.8 3.4 %fusion = bf16[1,512,1024]{2,1,0:T(8,128)(2,1)} fusion(bf16[512,1024]{1,0:T(8,128)(2,1)} %shard_map.73, bf16[1024,1024]{1,0:T(8,128)(2,1)S(1)} %copy-done), kind=kOutput, calls=%fused_computation.1 | convolution fusion | flops 1074266112 | bytes 4194304 | tf_op jit(solution)/shard_map/dot_general | solution.py:20
Async XLA Ops:
  0.0 77.8 %copy-start = (bf16[1024,1024]{1,0:T(8,128)(2,1)S(1)}, bf16[1024,1024]{1,0:T(8,128)(2,1)}, u32[]{:S(2)}) copy-start(bf16[1024,1024]{1,0:T(8,128)(2,1)} %param.12) | copy-start | bytes 6291460

commit v8 on v7

--- a/solution.py
+++ b/solution.py
@@ -12,7 +12,7 @@
 BLK = 128
 MESH = pl.DeviceIdType.MESH
 LAG = 1
-FIRST = 7
+FIRST = 5
 VPS = 4
 
 

time: 82.9 us -> 82.6 us (level)
  no operation moved by 1% of the time
where the time goes in v8:
time: 82.6 us; the launch traced here: 81 us
  Pallas kernels  77.5 us (94%)
  matrix products  3.45 us (4%)
    pallas_call x1, Pallas kernels, local(): pl.pallas_call(functools.partial(kernel, nview, ntok, math.isqrt(nview),...  77.5 us
    dot_general x1, matrix products, dot(): return jnp.dot(a, b, preferred_element_type=jnp.float32)  3.45 us

profile of v8, /device:TPU:33, one launch (start us, length us, event | category | flops | bytes accessed | tf_op | source)
XLA Modules:
  0.0 81.0 jit_solution(8200616151916894230)
XLA Ops:
  0.0 0.0 copy-start
  0.0 77.5 %shard_map.73 = bf16[512,1024]{1,0:T(8,128)(2,1)} custom-call(bf16[512,1024]{1,0:T(8,128)(2,1)} %bitcast.8, bf16[16,1024]{1,0:T(8,128)(2,1)} %cond_hbm.1, bf16[1024,1024]{1,0:T(8,128)(2,1)} %wq_hbm.1, bf16[1024,1024]{1,0:T(8,128)(2,1)} %wk_hbm.1, bf16[1024,1024]{1,0:T(8,128)(2,1)} %wv_hbm.1, s32[4,2,8]{2,1,0:T(2,128)} %bitcast.9), custom_call_target="tpu_custom_call" | custom-call | tf_op jit(solution)/shard_map/pallas_call | solution.py:430
  77.5 0.0 copy-done
  77.5 3.4 %fusion = bf16[1,512,1024]{2,1,0:T(8,128)(2,1)} fusion(bf16[512,1024]{1,0:T(8,128)(2,1)} %shard_map.73, bf16[1024,1024]{1,0:T(8,128)(2,1)S(1)} %copy-done), kind=kOutput, calls=%fused_computation.1 | convolution fusion | flops 1074266112 | bytes 4194304 | tf_op jit(solution)/shard_map/dot_general | solution.py:20
Async XLA Ops:
  0.0 77.5 %copy-start = (bf16[1024,1024]{1,0:T(8,128)(2,1)S(1)}, bf16[1024,1024]{1,0:T(8,128)(2,1)}, u32[]{:S(2)}) copy-start(bf16[1024,1024]{1,0:T(8,128)(2,1)} %param.12) | copy-start | bytes 6291460
